TPU v7x, 256 devices: a whole 4x4x8 slice. The times are simulated.
256 devices in a mesh: ctx: 16 (over x, y_hi, core), dec: 8 (over z), tp: 2 (over y_lo).
Axes of the slice: x: 4, y: 4 (y_hi: 2, y_lo: 2; y = y_hi * 2 + y_lo), z: 8, core: 2. Of those that a mesh axis runs over, the one named last changes fastest.
Arguments:
- queries: bfloat16 [8, 4096, 8192], P('dec', 'ctx', 'tp'), may hold values from -6 to 6
- keys: bfloat16 [8, 4096, 512], P('dec', 'ctx', 'tp'), may hold values from -6 to 6
- values: bfloat16 [8, 4096, 512], P('dec', 'ctx', 'tp'), may hold values from -6 to 6
- dec_queries: bfloat16 [4, 128, 8192], P(None, 'dec', 'tp'), may hold values from -6 to 6
- dec_keys: bfloat16 [4, 128, 512], P(None, 'dec', 'tp'), may hold values from -6 to 6
- dec_values: bfloat16 [4, 128, 512], P(None, 'dec', 'tp'), may hold values from -6 to 6
- page_table: int32 [8, 32], replicated, may hold values from 0 to 7
- ctx_lengths: int32 [128], P('dec'), may hold values from 1 to 4096, as said below
Outputs:
- prefill_out: bfloat16 [8, 4096, 8192], P('dec', 'ctx', 'tp')
- decode_out: bfloat16 [4, 128, 8192], P(None, 'dec', 'tp')
Inputs may be any that keep to these rules, and one draw needn't show every extreme that they name: Each decode group has a row with ctx_lengths equal to 4096.
All inputs are finite; a program needn't handle non-finite values.
Results may differ from a plain program's by a relative error of at most 0.02.
Values may be sent and summed in bfloat16 or wider, within the bound.
No kernel may reach another device: no remote copies, remote signals or barrier semaphores. Data moves between devices by JAX's collectives and lax.ppermute only.
A program may use at most 128 MiB of HBM per device.

v0:
```python
import functools

import jax
import jax.numpy as jnp
from jax import lax
from jax.experimental import pallas as pl
from jax.experimental.pallas import tpu as pltpu
from jax.sharding import PartitionSpec as P

HD = 128
PAGE = 128
SCALE = HD**-0.5
LOG2E = 1.4426950408889634
CEXP = SCALE * LOG2E
SAFE = 75.0
NEG = -1e30
NT = (((1,), (1,)), ((), ()))
VMEM_LIMIT = 56 * 2**20
SMALL_LIMIT = 16 * 2**20
F32 = jnp.float32
BF16 = jnp.bfloat16


def dot_nt(a, b):
    return lax.dot_general(a, b, NT, preferred_element_type=F32)


def dot_nn(a, b):
    return jnp.dot(a, b, preferred_element_type=F32)


def row_norm_bound(block, fold):
    sq = block.astype(F32)
    sq = sq * sq
    each = sq.shape[0] // fold
    most = sq[:each]
    for i in range(1, fold):
        most = jnp.maximum(most, sq[i * each : (i + 1) * each])
    return jnp.max(jnp.sum(most, axis=1, keepdims=True), axis=0, keepdims=True)


def prefill_kernel(meta, *refs, group, rows, first):
    chip, core, xpos, ypos = meta[0], meta[1], meta[2], meta[3]
    if first:
        q_own, q_oth, own, rr, ll, yy, state, flag, ks, vx, kbest, sem = refs
    else:
        q_own, q_oth, ry, ly, xx, xy, before_a, flag_a, before_b, flag_b = refs[:10]
        o_own, o_oth, ks, vx, kbest, acc, sem = refs[-7:]
    step = pl.program_id(0)
    half = 256

    def chip_id(dx, dy):
        return lax.rem(xpos + dx + 4, 4) * 2 + lax.rem(ypos + dy, 2)

    if first:
        pieces = [(chip_id(0, 0), own), (chip_id(-1, 0), rr), (chip_id(1, 0), ll), (chip_id(0, 1), yy)]
    else:
        pieces = [(chip_id(-1, 1), ry), (chip_id(1, 1), ly), (chip_id(2, 0), xx), (chip_id(2, 1), xy)]
    needed = [p[0] <= chip for p in pieces]
    slots, count = [], jnp.int32(0)
    for need in needed:
        slots.append(count)
        count = count + need.astype(jnp.int32)

    def copies(index):
        buf = pieces[index][1]
        base = slots[index] * 512
        out = []
        for side in range(2):
            off = side * 512
            dst = pl.multiple_of(base + side * half, half)
            out.append(
                pltpu.make_async_copy(
                    buf.at[pl.ds(off, half), :], ks.at[pl.ds(dst, half), :], sem.at[index, 2 * side]
                )
            )
            out.append(
                pltpu.make_async_copy(
                    buf.at[pl.ds(off + half, half), :],
                    vx.at[pl.ds(dst, half), pl.ds(0, HD)],
                    sem.at[index, 2 * side + 1],
                )
            )
        return out

    @pl.when(step == 0)
    def _load():
        for index in range(4):

            @pl.when(needed[index])
            def _start(index=index):
                for copy in copies(index):
                    copy.start()

        vx[:, HD:] = jnp.ones((vx.shape[0], HD), BF16)
        for index in range(4):

            @pl.when(needed[index])
            def _wait(index=index):
                for copy in copies(index):
                    copy.wait()

        def norm(block, best):
            return jnp.maximum(best, row_norm_bound(ks[pl.ds(pl.multiple_of(block * 512, 512), 512), :], 8))

        kbest[0:1, 0:1] = lax.fori_loop(0, count, norm, jnp.zeros((1, 1), F32))

    q_refs = (q_own, q_oth)
    qmax = jnp.zeros((1, 1), F32)
    for q_ref in q_refs:
        for g in range(group):
            qmax = jnp.maximum(qmax, row_norm_bound(q_ref[:, g * HD : (g + 1) * HD], 4))
    bound = qmax * kbest[0:1, 0:1] * (SCALE * SCALE * 1.0001)
    safe = bound[0, 0] <= SAFE * SAFE
    if first:
        flag[step] = jnp.where(safe, 0, 1)
    else:
        later = step >= flag_a.shape[0]
        shifted = jnp.where(later, flag_b[lax.rem(step, flag_b.shape[0])], flag_a[lax.rem(step, flag_a.shape[0])]) != 0
        safe = safe & jnp.logical_not(shifted)

    def tiles():
        for g in range(group):
            for side in range(2):
                for r in range(half // rows):
                    q = q_refs[side][r * rows : (r + 1) * rows, g * HD : (g + 1) * HD]
                    yield g, side, r, slice(side * half + r * rows, side * half + (r + 1) * rows), q

    def allowed(side, r):
        q_pos0 = (core if side == 0 else 1 - core) * half + r * rows
        row = lax.broadcasted_iota(jnp.int32, (rows, half), 0) + q_pos0
        col = lax.broadcasted_iota(jnp.int32, (rows, half), 1)
        return jnp.concatenate([col + core * half <= row, col + (1 - core) * half <= row], axis=1)

    def weighted(q, base, size, ok=None):
        p = jnp.exp2(dot_nt(q, ks[pl.ds(base, size), :]) * CEXP)
        if ok is not None:
            masked = jnp.where(ok, p[:, :512], 0.0)
            p = masked if size == 512 else jnp.concatenate([masked, p[:, 512:]], axis=1)
        return dot_nn(p.astype(BF16), vx[pl.ds(base, size), :])

    def write(g, side, at, both):
        cols = slice(g * HD, (g + 1) * HD)
        r = slice(at.start - side * half, at.stop - side * half)
        (o_own, o_oth)[side][r, cols] = (both[:, :HD] / both[:, HD:]).astype(BF16)

    full = count == 4

    def started(g, at):
        return jnp.where(later, before_b[g, at, :], before_a[g, at, :])


    @pl.when(safe & full)
    def _straight():
        for g, side, r, at, q in tiles():
            if first:
                state[g, at, :] = weighted(q, 0, 2048, allowed(side, r))
            else:
                write(g, side, at, started(g, at) + weighted(q, 0, 2048))

    @pl.when(safe & jnp.logical_not(full))
    def _plain():
        sums = state if first else acc
        for g, side, r, at, q in tiles():
            if first:
                sums[g, at, :] = weighted(q, 0, 512, allowed(side, r))
            else:
                sums[g, at, :] = started(g, at)

        def one(index, carry):
            for g, side, r, at, q in tiles():
                sums[g, at, :] += weighted(q, pl.multiple_of(index * 512, 512), 512)
            return carry

        lax.fori_loop(1 if first else 0, count, one, 0)
        if not first:
            for g, side, r, at, q in tiles():
                write(g, side, at, sums[g, at, :])

    @pl.when(jnp.logical_not(safe))
    def _online():
        sums = state if first else acc
        lane = lax.broadcasted_iota(jnp.int32, (rows, 2 * HD), 1)
        for g, side, r, at, q in tiles():
            if first:
                sums[g, at, :] = jnp.zeros((rows, 2 * HD), F32)
                best0 = jnp.full((rows, 1), NEG, F32)
            else:
                old = started(g, at)
                sums[g, at, :] = jnp.where(lane >= HD, old[:, HD : HD + 1], old)
                best0 = jnp.where(shifted, old[:, 2 * HD - 1 :], 0.0)
            own_ok = allowed(side, r) if first else None

            def one(index, best, q=q, g=g, at=at, own_ok=own_ok):
                base = pl.multiple_of(index * 512, 512)
                s = dot_nt(q, ks[pl.ds(base, 512), :]) * SCALE
                if own_ok is not None:
                    s = jnp.where(jnp.logical_or(own_ok, index > 0), s, NEG)
                new = jnp.maximum(best, jnp.max(s, axis=1, keepdims=True))
                p = jnp.exp(s - new)
                if own_ok is not None:
                    p = jnp.where(jnp.logical_or(own_ok, index > 0), p, 0.0)
                sums[g, at, :] = sums[g, at, :] * jnp.exp(best - new) + dot_nn(
                    p.astype(BF16), vx[pl.ds(base, 512), :]
                )
                return new

            best = lax.fori_loop(0, count, one, best0)
            if first:
                sums[g, at, :] = jnp.where(lane == 2 * HD - 1, best, sums[g, at, :])
            else:
                write(g, side, at, sums[g, at, :])


def prefill(meta, queries, q_oth, bufs, head, heads, before=None, group=4, rows=128):
    per = 16 // group
    at = head // group
    first = before is None
    steps = heads // group
    any_spec = pl.BlockSpec(memory_space=pl.ANY)
    smem = pl.BlockSpec(memory_space=pltpu.SMEM)
    state_shape = (group, 512, 2 * HD)
    in_specs = [
        pl.BlockSpec((256, group * HD), lambda i, m: (0, m[1] * per + at + i)),
        pl.BlockSpec((256, group * HD), lambda i, m: (0, at + i)),
    ] + [any_spec] * len(bufs)
    args = [queries, q_oth, *bufs]
    scratch = [pltpu.VMEM((2048, HD), BF16), pltpu.VMEM((2048, 2 * HD), BF16), pltpu.VMEM((8, HD), F32)]
    if first:
        out_specs = [pl.BlockSpec(state_shape, lambda i, m: (i, 0, 0)), smem]
        out_shape = [
            jax.ShapeDtypeStruct((heads,) + state_shape[1:], F32),
            jax.ShapeDtypeStruct((steps,), jnp.int32),
        ]
    else:
        (sums_a, flags_a), (sums_b, flags_b) = before
        split = sums_a.shape[0] // group
        in_specs += [
            pl.BlockSpec(state_shape, lambda i, m: (jnp.minimum(i, split - 1), 0, 0)),
            smem,
            pl.BlockSpec(state_shape, lambda i, m: (jnp.maximum(i - split, 0), 0, 0)),
            smem,
        ]
        args += [sums_a, flags_a, sums_b, flags_b]
        out_specs = [pl.BlockSpec((256, group * HD), lambda i, m: (0, i))] * 2
        out_shape = [jax.ShapeDtypeStruct((256, heads * HD), BF16)] * 2
        scratch.append(pltpu.VMEM(state_shape, F32))
    scratch.append(pltpu.SemaphoreType.DMA((4, 4)))
    return pl.pallas_call(
        functools.partial(prefill_kernel, group=group, rows=rows, first=first),
        grid_spec=pltpu.PrefetchScalarGridSpec(
            num_scalar_prefetch=1,
            grid=(steps,),
            in_specs=in_specs,
            out_specs=out_specs,
            scratch_shapes=scratch,
        ),
        out_shape=out_shape,
        compiler_params=pltpu.CompilerParams(vmem_limit_bytes=VMEM_LIMIT),
        cost_estimate=pl.CostEstimate(
            flops=8 * 512 * heads * 2048 * HD, bytes_accessed=4 * 2**20, transcendentals=0
        ),
        name="prefill_a" if first else "prefill_b",
    )(meta, *args)


def join_kernel(meta, *refs):
    parts, out, sem = refs[:-2], refs[-2], refs[-1]
    copies = []
    for side in range(2):
        at = (meta[1] if side == 0 else 1 - meta[1]) * 16 * HD
        for part in parts[side * len(parts) // 2 : (side + 1) * len(parts) // 2]:
            wide = part.shape[1]
            copies.append(
                pltpu.make_async_copy(part, out.at[:, pl.ds(pl.multiple_of(at, HD), wide)], sem.at[len(copies)])
            )
            at = at + wide
    for copy in copies:
        copy.start()
    for copy in copies:
        copy.wait()


def join(meta, own, oth):
    parts = [*own, *oth]
    return pl.pallas_call(
        join_kernel,
        grid_spec=pltpu.PrefetchScalarGridSpec(
            num_scalar_prefetch=1,
            grid=(1,),
            in_specs=[pl.BlockSpec(part.shape, lambda i, m: (0, 0)) for part in parts],
            out_specs=pl.BlockSpec(memory_space=pl.ANY),
            scratch_shapes=[pltpu.SemaphoreType.DMA((len(parts),))],
        ),
        out_shape=jax.ShapeDtypeStruct((256, 32 * HD), BF16),
        compiler_params=pltpu.CompilerParams(vmem_limit_bytes=SMALL_LIMIT),
        name="join",
    )(meta, *parts)


def decode_kernel(
    meta, table, q_ref, nk_ref, nv_ref, len_ref, own, f1, f2, f3, f4, b1, b2, b3,
    keep, send, ks, vx, sem,
):
    chip, core, zpos, mask = meta[0], meta[1], meta[4], meta[5]
    sources = {0: own, 7: f1, 6: f2, 5: f3, 4: f4, 1: b1, 2: b2, 3: b3}

    def page_copy(buf, off, page):
        return (
            pltpu.make_async_copy(
                buf.at[pl.ds(off, PAGE), :], ks.at[pl.ds(page * PAGE, PAGE), :], sem.at[page, 0]
            ),
            pltpu.make_async_copy(
                buf.at[pl.ds(off + 256, PAGE), :],
                vx.at[pl.ds(page * PAGE, PAGE), pl.ds(0, HD)],
                sem.at[page, 1],
            ),
        )

    for page in range(4):
        side, inner = page // 2, page % 2
        from_core = core if side == 0 else 1 - core
        prompt = table[zpos, chip * 4 + from_core * 2 + inner]
        rel = lax.rem(prompt - zpos + 8, 8)
        for r in range(8):
            buf, off = sources[r], side * 512 + inner * PAGE

            @pl.when(rel == r)
            def _start(buf=buf, off=off, page=page):
                for copy in page_copy(buf, off, page):
                    copy.start()

    vx[:, HD:] = jnp.ones((512 + 64, HD), BF16)
    ks[512:, :] = nk_ref[...].reshape(64, HD)
    vx[512:, :HD] = nv_ref[...].reshape(64, HD)
    for page in range(4):
        for copy in page_copy(own, 0, page):
            copy.wait()

    lens = len_ref[...]
    row = lax.broadcasted_iota(jnp.int32, (64, 64), 0)
    col = lax.broadcasted_iota(jnp.int32, (64, 64), 1)
    new_ok = (lax.rem(row, 16) == lax.rem(col, 16)) & (col <= row) & (chip == 0)
    pos = lax.broadcasted_iota(jnp.int32, (64, 256), 1)
    base = chip * 512
    ok0 = pos + (base + core * 256) < lens
    ok1 = pos + (base + (1 - core) * 256) < lens
    ok = jnp.concatenate([ok0, ok1, new_ok], axis=1)
    keys = ks[...]
    vals = vx[...]
    lane = lax.broadcasted_iota(jnp.int32, (64, HD), 1)
    for part, out in enumerate((keep, send)):
        stats = jnp.zeros((64, HD), F32)
        for g0 in range(0, 8, 4):
            qs = []
            for g in range(g0, g0 + 4):
                head = (part * 8 + g) ^ mask
                qs.append(q_ref[:, :, pl.ds(pl.multiple_of(head * HD, HD), HD)].reshape(64, HD))
            s = dot_nt(jnp.concatenate(qs, axis=0), keys) * SCALE
            s = jnp.where(jnp.concatenate([ok] * 4, axis=0), s, NEG)
            best = jnp.max(s, axis=1, keepdims=True).astype(BF16).astype(F32)
            p = jnp.exp(s - jnp.maximum(best, 0.5 * NEG)).astype(BF16)
            o = dot_nn(p, vals)
            for i in range(4):
                g = g0 + i
                at = slice(i * 64, (i + 1) * 64)
                out[:, g * HD : (g + 1) * HD] = o[at, :HD].astype(BF16)
                total = o[at, HD:]
                high = total.astype(BF16).astype(F32)
                stats = jnp.where(lane == g, best[at], stats)
                stats = jnp.where(lane == 16 + g, high, stats)
                stats = jnp.where(lane == 32 + g, total - high, stats)
        out[:, 8 * HD :] = stats.astype(BF16)


def decode_part(meta, table, dec_q, dec_k, dec_v, lens, bufs):
    any_spec = pl.BlockSpec(memory_space=pl.ANY)
    shape = jax.ShapeDtypeStruct((64, 9 * HD), BF16)
    return pl.pallas_call(
        decode_kernel,
        grid_spec=pltpu.PrefetchScalarGridSpec(
            num_scalar_prefetch=2,
            grid=(1,),
            in_specs=[
                pl.BlockSpec((4, 16, 16 * HD), lambda i, m, t: (0, 0, m[1])),
                pl.BlockSpec((4, 16, HD), lambda i, m, t: (0, 0, m[1])),
                pl.BlockSpec((4, 16, HD), lambda i, m, t: (0, 0, m[1])),
                pl.BlockSpec((64, 1), lambda i, m, t: (0, 0)),
            ]
            + [any_spec] * 8,
            out_specs=[pl.BlockSpec((64, 9 * HD), lambda i, m, t: (0, 0))] * 2,
            scratch_shapes=[
                pltpu.VMEM((512 + 64, HD), BF16),
                pltpu.VMEM((512 + 64, 2 * HD), BF16),
                pltpu.SemaphoreType.DMA((4, 2)),
            ],
        ),
        out_shape=[shape, shape],
        compiler_params=pltpu.CompilerParams(vmem_limit_bytes=SMALL_LIMIT),
        cost_estimate=pl.CostEstimate(flops=2 * 10**9, bytes_accessed=2**20, transcendentals=0),
        name="decode_part",
    )(meta, table, dec_q, dec_k, dec_v, lens, *bufs)


def merge_kernel(*refs, count, heads, last):
    ins, outs = refs[:count], refs[count:]
    cols = heads * HD
    lane = lax.broadcasted_iota(jnp.int32, (64, HD), 1)
    stats_in = [ref[:, cols:].astype(F32) for ref in ins]

    def total_of(stat):
        return pltpu.roll(stat, HD - 16, 1) + pltpu.roll(stat, HD - 32, 1)

    best = functools.reduce(jnp.maximum, stats_in)
    shares = [jnp.exp(stat - best) for stat in stats_in]
    total = sum(total_of(stat) * w for stat, w in zip(stats_in, shares))
    used = lane < heads
    if last:
        inverse = 1.0 / jnp.where(used, total, 1.0)
        shares = [w * inverse for w in shares]
    place = lax.broadcasted_iota(jnp.int32, (HD, cols), 0) == (
        lax.broadcasted_iota(jnp.int32, (HD, cols), 1) // HD
    )
    place = place.astype(BF16)

    def spread(w):
        w = jnp.where(used, w, 0.0)
        high = w.astype(BF16)
        low = (w - high.astype(F32)).astype(BF16)
        return dot_nn(high, place) + dot_nn(low, place)

    joined = sum(ref[:, :cols].astype(F32) * spread(w) for ref, w in zip(ins, shares))
    if last:
        outs[0][...] = joined.astype(BF16)
        return
    high = total.astype(BF16).astype(F32)
    low = total - high
    each = heads // len(outs)
    for part, out in enumerate(outs):
        first = part * each
        out[:, : each * HD] = joined[:, first * HD : (first + each) * HD].astype(BF16)
        stats = jnp.zeros((64, HD), F32)
        for values, goal in ((best, 0), (high, 16), (low, 32)):
            turn = (goal - first) % HD
            moved = pltpu.roll(values, turn, 1) if turn else values
            stats = jnp.where((lane >= goal) & (lane < goal + each), moved, stats)
        out[:, each * HD :] = stats.astype(BF16)


def merge(parts, heads, runs, last=False):
    width = heads * HD if last else (heads // runs + 1) * HD
    return pl.pallas_call(
        functools.partial(merge_kernel, count=len(parts), heads=heads, last=last),
        out_shape=[jax.ShapeDtypeStruct((64, width), BF16)] * runs,
        cost_estimate=pl.CostEstimate(flops=10**6, bytes_accessed=2**18, transcendentals=0),
        name="merge",
    )(*parts)


def place_kernel(meta, *refs):
    parts, out, sem = refs[:4], refs[4], refs[5]
    core, mask = meta[1], meta[5]
    copies = []
    for index, ref in enumerate(parts):
        which = core if index < 2 else 1 - core
        for b in range(4):
            at = pl.multiple_of((which * 16 + ((index % 2 * 8 + 2 * b) ^ mask)) * HD, 2 * HD)
            copies.append(
                pltpu.make_async_copy(
                    ref.at[:, :, b * 2 * HD : (b + 1) * 2 * HD], out.at[:, :, pl.ds(at, 2 * HD)], sem.at[index, b]
                )
            )
    for copy in copies:
        copy.start()
    for copy in copies:
        copy.wait()


def place(meta, parts):
    return pl.pallas_call(
        place_kernel,
        in_specs=[pl.BlockSpec(memory_space=pltpu.SMEM)] + [pl.BlockSpec(memory_space=pltpu.VMEM)] * 4,
        out_specs=pl.BlockSpec(memory_space=pl.ANY),
        scratch_shapes=[pltpu.SemaphoreType.DMA((4, 4))],
        out_shape=jax.ShapeDtypeStruct((4, 16, 4096), BF16),
        name="place",
    )(meta, *[part.reshape(4, 16, 1024) for part in parts])


def ctx_move(array, dx=0, flip_y=0, flip_core=0, mirror_x=0):
    pairs = []
    for c in range(16):
        x, y, core = c // 4, (c // 2) % 2, c % 2
        to_x = ((x + dx) % 4) ^ mirror_x
        pairs.append((c, to_x * 4 + (y ^ flip_y) * 2 + (core ^ flip_core)))
    return lax.ppermute(array, "ctx", pairs)


def dec_move(array, dz):
    return lax.ppermute(array, "dec", [(i, (i + dz) % 8) for i in range(8)])


def body(queries, keys, values, dec_queries, dec_keys, dec_values, page_table, ctx_lengths):
    c = lax.axis_index("ctx")
    z = lax.axis_index("dec")
    x, y, core = c // 4, (c // 2) % 2, c % 2
    chip = c // 2
    mask = y * 8 + x * 2
    meta = jnp.stack([chip, core, x, y, z, mask]).astype(jnp.int32)

    k0, v0 = keys[0], values[0]
    first = jnp.concatenate([k0[:, :HD], v0[:, :HD]], axis=0)
    second = jnp.concatenate([k0[:, HD:], v0[:, HD:]], axis=0)
    mine = jnp.where(core == 0, first, second)
    other = jnp.where(core == 0, second, first)
    q_send = lax.dynamic_slice_in_dim(queries[0], (1 - core) * 2048, 2048, 1)
    barrier = lax.optimization_barrier
    got, q_oth = barrier((ctx_move(other, flip_core=1), ctx_move(q_send, flip_core=1)))
    chunk = jnp.concatenate([mine, got], axis=0)
    lens = jnp.tile(ctx_lengths, 4)[:, None]

    q = queries[0]
    f1, b1 = dec_move(chunk, 1), dec_move(chunk, -1)
    rr, ll, yy = ctx_move(chunk, dx=1), ctx_move(chunk, dx=-1), ctx_move(chunk, flip_y=1)
    f1, b1, rr, ll, yy = barrier((f1, b1, rr, ll, yy))
    near = (chunk, rr, ll, yy)
    f2, b2 = dec_move(f1, 1), dec_move(b1, -1)
    ry, ly = ctx_move(yy, dx=1), ctx_move(yy, dx=-1)
    pa0 = prefill(meta, q, q_oth, near, 0, 8)
    f2, b2, ry, ly, pa0 = barrier((f2, b2, ry, ly, pa0))
    f3, b3, f4 = dec_move(f2, 1), dec_move(b2, -1), dec_move(f2, 2)
    xx, xy = ctx_move(rr, dx=1), ctx_move(ly, dx=-1)
    pa1 = prefill(meta, q, q_oth, near, 8, 8)
    f3, b3, f4, xx, xy, pa1 = barrier((f3, b3, f4, xx, xy, pa1))
    far = (ry, ly, xx, xy)

    keep, send = decode_part(
        meta, page_table, dec_queries, dec_keys, dec_values, lens, (chunk, f1, f2, f3, f4, b1, b2, b3)
    )
    got = ctx_move(send, flip_y=1)
    own_out, oth_out = prefill(meta, q, q_oth, far, 0, 16, (pa0, pa1))
    got, own_out, oth_out = barrier((got, own_out, oth_out))
    back = ctx_move(oth_out, flip_core=1)
    keep, *send = merge((keep, got), 8, 4)
    got = [ctx_move(send[k - 1], mirror_x=k) for k in (1, 2, 3)]
    got, back = barrier((got, back))
    (part,) = merge((keep, *got), 2, 1, last=True)
    got = [ctx_move(part, mirror_x=k) for k in (1, 2, 3)]
    prefill_out = join(meta, [own_out], [back])
    got, prefill_out = barrier((got, prefill_out))
    part = jnp.concatenate([part, *got], axis=1)
    decode_out = place(
        meta,
        [part, ctx_move(part, flip_y=1), ctx_move(part, flip_core=1), ctx_move(part, flip_y=1, flip_core=1)],
    )
    return (prefill_out[None], decode_out)


def solution(mesh):
    return jax.shard_map(
        body,
        mesh=mesh,
        in_specs=(
            P("dec", "ctx", "tp"),
            P("dec", "ctx", "tp"),
            P("dec", "ctx", "tp"),
            P(None, "dec", "tp"),
            P(None, "dec", "tp"),
            P(None, "dec", "tp"),
            P(),
            P("dec"),
        ),
        out_specs=(P("dec", "ctx", "tp"), P(None, "dec", "tp")),
        check_vma=False,
    )
```

profile of v0, /device:TPU:1, one launch (start us, length us, event | category | flops | bytes accessed | tf_op | source)
XLA Modules:
  0.0 368.1 jit_solution(12803068849342954605)
XLA Ops:
  0.7 1.4 dynamic-slice_bitcast_fusion
  2.1 3.3 collective-permute-start.1
  5.5 0.1 broadcast_select_fusion.1
  5.5 0.1 collective-permute-start
  5.6 2.2 collective-permute-done
  7.9 0.1 collective-permute-start.2
  8.0 3.9 %collective-permute-start.3 = (bf16[1024,128]{1,0:T(8,128)(2,1)S(1)}, bf16[1024,128]{1,0:T(8,128)(2,1)S(1)}, u32[]{:S(2)}, u32[]{:S(2)}) collective-permute-start(bf16[1024,128]{1,0:T(8,128)(2,1)S(1)} %pad_maximum_fusion.refs_2_.own), channel_id=1, source_target_pairs={{0,14},{2,0},{4,2},{6,4},{8,6},{10,8},{12,10},{14,12},{1,15},{3,1}... | collective-permute-start | bytes 786440 | tf_op jit(solution)/shard_map/ppermute | solution.py:500
  11.9 1.2 collective-permute-start.4
  13.1 1.5 collective-permute-start.5
  14.6 2.9 collective-permute-start.6
  17.5 0.1 broadcast_in_dim_tile.4.len_ref
  17.6 0.6 stack.27.meta
  18.2 0.0 collective-permute-done.2.f1
  18.2 0.0 collective-permute-done.3.b1
  18.2 2.1 collective-permute-done.4.refs_3_
  20.3 0.0 collective-permute-done.5.refs_4_
  20.3 2.3 collective-permute-done.6.refs_5_
  22.7 2.7 collective-permute-start.10
  25.4 0.0 collective-permute-start.7
  25.4 2.7 collective-permute-start.8
  28.0 0.2 collective-permute-start.14
  28.3 21.0 %prefill_a.2 = (f32[8,512,256]{2,1,0:T(8,128)}, s32[2]{0:T(128)}) custom-call(s32[6]{0:T(128)} %stack.27.meta, bf16[256,4096]{1,0:T(8,128)(2,1)} %bitcast.17, bf16[256,2048]{1,0:T(8,128)(2,1)} %copy-done.22, bf16[1024,128]{1,0:T(8,128)(2,1)} %copy-done.1, bf16[1024,128]{1,0:T(8,128)(2,1)} %copy-done.23, bf16[1024,128]{1,0:T(8,128)(2,1)} %copy-done.24, ...), custom_call_target="tpu_custom_call" | custom-call | flops 8589934592 | bytes 4194304 | tf_op jit(solution)/shard_map/prefill_a/pallas_call | solution.py:249
  49.3 0.0 collective-permute-done.7.f2
  49.3 0.0 collective-permute-done.8.b2
  49.3 0.0 copy-start.26
  49.3 0.0 collective-permute-done.10.refs_3_
  49.3 0.0 copy-start.6
  49.3 0.0 copy-start.7
  49.4 0.0 copy-start.8
  49.4 0.0 copy-start.9
  49.4 0.1 collective-permute-start.11
  49.5 1.5 collective-permute-start.13
  51.0 1.1 collective-permute-start.12
  52.1 34.3 %collective-permute-start.15 = (bf16[1024,128]{1,0:T(8,128)(2,1)S(1)}, bf16[1024,128]{1,0:T(8,128)(2,1)S(1)}, u32[]{:S(2)}, u32[]{:S(2)}) collective-permute-start(bf16[1024,128]{1,0:T(8,128)(2,1)S(1)} %collective-permute-done.10.refs_3_), channel_id=1, source_target_pairs={{0,192},{16,208},{32,224},{48,240},{64,0},{80,16},{96,32},{112,48}... | collective-permute-start | bytes 786440 | tf_op jit(solution)/shard_map/ppermute | solution.py:496
  86.4 21.0 %prefill_a.3 = (f32[8,512,256]{2,1,0:T(8,128)}, s32[2]{0:T(128)}) custom-call(s32[6]{0:T(128)} %stack.27.meta, bf16[256,4096]{1,0:T(8,128)(2,1)} %bitcast.18, bf16[256,2048]{1,0:T(8,128)(2,1)} %copy-done.22, bf16[1024,128]{1,0:T(8,128)(2,1)} %copy-done.1, bf16[1024,128]{1,0:T(8,128)(2,1)} %copy-done.23, bf16[1024,128]{1,0:T(8,128)(2,1)} %copy-done.24, ...), custom_call_target="tpu_custom_call" | custom-call | flops 8589934592 | bytes 4194304 | tf_op jit(solution)/shard_map/prefill_a/pallas_call | solution.py:249
  107.4 0.0 collective-permute-done.14.refs_4_
  107.5 0.0 collective-permute-done.13.f4
  107.5 0.0 collective-permute-done.15.refs_5_
  107.6 3.0 decode_part.1
  110.6 0.6 copy-done.3
  111.2 34.1 %collective-permute-start.16 = (bf16[64,1152]{1,0:T(8,128)(2,1)S(1)}, bf16[64,1152]{1,0:T(8,128)(2,1)S(1)}, u32[]{:S(2)}, u32[]{:S(2)}) collective-permute-start(bf16[64,1152]{1,0:T(8,128)(2,1)S(1)} %get-tuple-element.63), channel_id=1, source_target_pairs={{0,32},{16,48},{32,0},{48,16},{64,96},{80,112},{96,64},{112,80},{1... | collective-permute-start | bytes 442376 | tf_op jit(solution)/shard_map/ppermute | solution.py:496
  145.4 11.6 %prefill_b.1 = (bf16[256,2048]{1,0:T(8,128)(2,1)}, bf16[256,2048]{1,0:T(8,128)(2,1)}) custom-call(s32[6]{0:T(128)} %stack.27.meta, bf16[256,4096]{1,0:T(8,128)(2,1)} %bitcast.19, bf16[256,2048]{1,0:T(8,128)(2,1)} %copy-done.22, bf16[1024,128]{1,0:T(8,128)(2,1)} %copy-done.26, bf16[1024,128]{1,0:T(8,128)(2,1)} %copy-done.27, bf16[1024,128]{1,0:T(8,128)(2,1)} %copy-done.28, ...), custom_call_target="tpu_custom_call" | custom-call | flops 17179869184 | bytes 4194304 | tf_op jit(solution)/shard_map/prefill_b/pallas_call | solution.py:249
  157.0 0.0 copy-start.11
  157.0 5.0 %collective-permute-start.20 = (bf16[256,2048]{1,0:T(8,128)(2,1)}, bf16[256,2048]{1,0:T(8,128)(2,1)S(1)}, u32[]{:S(2)}, u32[]{:S(2)}) collective-permute-start(bf16[256,2048]{1,0:T(8,128)(2,1)} %get-tuple-element.78), channel_id=1, source_target_pairs={{0,16},{16,0},{32,48},{48,32},{64,80},{80,64},{96,112},{112,96},{1... | collective-permute-start | bytes 3145736 | tf_op jit(solution)/shard_map/ppermute | solution.py:496
  162.0 1.9 merge.2
  163.9 33.9 %collective-permute-start.17 = (bf16[64,384]{1,0:T(8,128)(2,1)}, bf16[64,384]{1,0:T(8,128)(2,1)S(1)}, u32[]{:S(2)}, u32[]{:S(2)}) collective-permute-start(bf16[64,384]{1,0:T(8,128)(2,1)} %get-tuple-element.75), channel_id=1, source_target_pairs={{0,64},{16,80},{32,96},{48,112},{64,0},{80,16},{96,32},{112,48},{1... | collective-permute-start | bytes 147464 | tf_op jit(solution)/shard_map/ppermute | solution.py:496
  197.8 142.1 %collective-permute-start.18 = (bf16[64,384]{1,0:T(8,128)(2,1)}, bf16[64,384]{1,0:T(8,128)(2,1)S(1)}, u32[]{:S(2)}, u32[]{:S(2)}) collective-permute-start(bf16[64,384]{1,0:T(8,128)(2,1)} %get-tuple-element.76), channel_id=1, source_target_pairs={{0,128},{16,144},{32,160},{48,176},{64,192},{80,208},{96,224},{112... | collective-permute-start | bytes 147464 | tf_op jit(solution)/shard_map/ppermute | solution.py:496
  340.0 0.0 collective-permute-start.19
  340.0 0.0 collective-permute-done.17.refs_1_
  340.0 2.5 collective-permute-done.18.refs_2_
  342.5 1.9 collective-permute-done.19.refs_3_
  344.4 0.6 copy-done.20
  345.0 1.8 merge.3
  346.7 0.0 collective-permute-start.21
  346.7 1.6 collective-permute-start.22
  348.4 2.2 collective-permute-start.23
  350.6 1.2 copy-done
  351.8 1.9 join.1
  353.8 0.1 collective-permute-start.24
  353.9 3.0 collective-permute-start.25
  356.9 3.0 collective-permute-start.26
  359.9 5.3 %collective-permute-done.26 = bf16[64,1024]{1,0:T(8,128)(2,1)S(1)} collective-permute-done((bf16[64,1024]{1,0:T(8,128)(2,1)S(1)}, bf16[64,1024]{1,0:T(8,128)(2,1)S(1)}, u32[]{:S(2)}, u32[]{:S(2)}) %collective-permute-start.26) | collective-permute-done | bytes 131104 | tf_op jit(solution)/shard_map/ppermute | solution.py:496
  365.2 0.6 copy-done.17
  365.8 2.0 place.1
  (66 shorter events, 0.2 us)
Async XLA Ops:
  0.6 4.8 %copy-start.12 = (bf16[1,256,256]{2,1,0:T(8,128)(2,1)S(1)}, bf16[1,256,256]{2,1,0:T(8,128)(2,1)}, u32[]{:S(2)}) copy-start(bf16[1,256,256]{2,1,0:T(8,128)(2,1)} %param.9) | copy-start | bytes 393220
  0.6 4.8 %copy-start.13 = (bf16[1,256,256]{2,1,0:T(8,128)(2,1)S(1)}, bf16[1,256,256]{2,1,0:T(8,128)(2,1)}, u32[]{:S(2)}) copy-start(bf16[1,256,256]{2,1,0:T(8,128)(2,1)} %param.10) | copy-start | bytes 393220
  0.7 16.9 %copy-start.21 = (s32[16]{0:T(128)S(1)}, s32[16]{0:T(128)}, u32[]{:S(2)}) copy-start(s32[16]{0:T(128)} %param.15) | copy-start | bytes 196
  2.1 5.8 %collective-permute-start.1 = (bf16[256,2048]{1,0:T(8,128)(2,1)S(1)}, bf16[256,2048]{1,0:T(8,128)(2,1)S(1)}, u32[]{:S(2)}, u32[]{:S(2)}) collective-permute-start(bf16[256,2048]{1,0:T(8,128)(2,1)S(1)} %dynamic-slice_bitcast_fusion), channel_id=1, source_target_pairs={{0,16},{16,0},{32,48},{48,32},{64,80},{80,64},{96,112},{112,96},{1... | collective-permute-start | bytes 3145736 | tf_op jit(solution)/shard_map/ppermute | solution.py:496
  5.5 2.4 collective-permute-start
  7.9 20.3 %copy-start.22 = (bf16[256,2048]{1,0:T(8,128)(2,1)}, bf16[256,2048]{1,0:T(8,128)(2,1)S(1)}, u32[]{:S(2)}) copy-start(bf16[256,2048]{1,0:T(8,128)(2,1)S(1)} %collective-permute-done.1.refs_1_) | copy-start | bytes 3145732
  7.9 20.3 %copy-start.1 = (bf16[1024,128]{1,0:T(8,128)(2,1)}, bf16[1024,128]{1,0:T(8,128)(2,1)S(1)}, u32[]{:S(2)}) copy-start(bf16[1024,128]{1,0:T(8,128)(2,1)S(1)} %pad_maximum_fusion.refs_2_.own) | copy-start | bytes 786436
  7.9 10.3 %collective-permute-start.2 = (bf16[1024,128]{1,0:T(8,128)(2,1)S(1)}, bf16[1024,128]{1,0:T(8,128)(2,1)S(1)}, u32[]{:S(2)}, u32[]{:S(2)}) collective-permute-start(bf16[1024,128]{1,0:T(8,128)(2,1)S(1)} %pad_maximum_fusion.refs_2_.own), channel_id=1, source_target_pairs={{0,2},{2,4},{4,6},{6,8},{8,10},{10,12},{12,14},{14,0},{1,3},{3,5},... | collective-permute-start | bytes 786440 | tf_op jit(solution)/shard_map/ppermute | solution.py:500
  8.0 10.2 %collective-permute-start.3 = (bf16[1024,128]{1,0:T(8,128)(2,1)S(1)}, bf16[1024,128]{1,0:T(8,128)(2,1)S(1)}, u32[]{:S(2)}, u32[]{:S(2)}) collective-permute-start(bf16[1024,128]{1,0:T(8,128)(2,1)S(1)} %pad_maximum_fusion.refs_2_.own), channel_id=1, source_target_pairs={{0,14},{2,0},{4,2},{6,4},{8,6},{10,8},{12,10},{14,12},{1,15},{3,1}... | collective-permute-start | bytes 786440 | tf_op jit(solution)/shard_map/ppermute | solution.py:500
  11.9 8.4 %collective-permute-start.4 = (bf16[1024,128]{1,0:T(8,128)(2,1)S(1)}, bf16[1024,128]{1,0:T(8,128)(2,1)S(1)}, u32[]{:S(2)}, u32[]{:S(2)}) collective-permute-start(bf16[1024,128]{1,0:T(8,128)(2,1)S(1)} %pad_maximum_fusion.refs_2_.own), channel_id=1, source_target_pairs={{0,64},{16,80},{32,96},{48,112},{64,128},{80,144},{96,160},{112,17... | collective-permute-start | bytes 786440 | tf_op jit(solution)/shard_map/ppermute | solution.py:496
  13.1 7.2 %collective-permute-start.5 = (bf16[1024,128]{1,0:T(8,128)(2,1)S(1)}, bf16[1024,128]{1,0:T(8,128)(2,1)S(1)}, u32[]{:S(2)}, u32[]{:S(2)}) collective-permute-start(bf16[1024,128]{1,0:T(8,128)(2,1)S(1)} %pad_maximum_fusion.refs_2_.own), channel_id=1, source_target_pairs={{0,192},{16,208},{32,224},{48,240},{64,0},{80,16},{96,32},{112,48}... | collective-permute-start | bytes 786440 | tf_op jit(solution)/shard_map/ppermute | solution.py:496
  14.6 8.1 %collective-permute-start.6 = (bf16[1024,128]{1,0:T(8,128)(2,1)S(1)}, bf16[1024,128]{1,0:T(8,128)(2,1)S(1)}, u32[]{:S(2)}, u32[]{:S(2)}) collective-permute-start(bf16[1024,128]{1,0:T(8,128)(2,1)S(1)} %pad_maximum_fusion.refs_2_.own), channel_id=1, source_target_pairs={{0,32},{16,48},{32,0},{48,16},{64,96},{80,112},{96,64},{112,80},{1... | collective-permute-start | bytes 786440 | tf_op jit(solution)/shard_map/ppermute | solution.py:496
  20.3 7.9 %copy-start.23 = (bf16[1024,128]{1,0:T(8,128)(2,1)}, bf16[1024,128]{1,0:T(8,128)(2,1)S(1)}, u32[]{:S(2)}) copy-start(bf16[1024,128]{1,0:T(8,128)(2,1)S(1)} %collective-permute-done.4.refs_3_) | copy-start | bytes 786436
  20.3 7.9 %copy-start.24 = (bf16[1024,128]{1,0:T(8,128)(2,1)}, bf16[1024,128]{1,0:T(8,128)(2,1)S(1)}, u32[]{:S(2)}) copy-start(bf16[1024,128]{1,0:T(8,128)(2,1)S(1)} %collective-permute-done.5.refs_4_) | copy-start | bytes 786436
  22.7 5.6 %copy-start.25 = (bf16[1024,128]{1,0:T(8,128)(2,1)}, bf16[1024,128]{1,0:T(8,128)(2,1)S(1)}, u32[]{:S(2)}) copy-start(bf16[1024,128]{1,0:T(8,128)(2,1)S(1)} %collective-permute-done.6.refs_5_) | copy-start | bytes 786436
  22.7 26.6 %collective-permute-start.9 = (bf16[1024,128]{1,0:T(8,128)(2,1)S(1)}, bf16[1024,128]{1,0:T(8,128)(2,1)S(1)}, u32[]{:S(2)}, u32[]{:S(2)}) collective-permute-start(bf16[1024,128]{1,0:T(8,128)(2,1)S(1)} %collective-permute-done.6.refs_5_), channel_id=1, source_target_pairs={{0,64},{16,80},{32,96},{48,112},{64,128},{80,144},{96,160},{112,17... | collective-permute-start | bytes 786440 | tf_op jit(solution)/shard_map/ppermute | solution.py:496
  22.7 26.6 %collective-permute-start.10 = (bf16[1024,128]{1,0:T(8,128)(2,1)S(1)}, bf16[1024,128]{1,0:T(8,128)(2,1)S(1)}, u32[]{:S(2)}, u32[]{:S(2)}) collective-permute-start(bf16[1024,128]{1,0:T(8,128)(2,1)S(1)} %collective-permute-done.6.refs_5_), channel_id=1, source_target_pairs={{0,192},{16,208},{32,224},{48,240},{64,0},{80,16},{96,32},{112,48}... | collective-permute-start | bytes 786440 | tf_op jit(solution)/shard_map/ppermute | solution.py:496
  25.4 23.9 %collective-permute-start.7 = (bf16[1024,128]{1,0:T(8,128)(2,1)S(1)}, bf16[1024,128]{1,0:T(8,128)(2,1)S(1)}, u32[]{:S(2)}, u32[]{:S(2)}) collective-permute-start(bf16[1024,128]{1,0:T(8,128)(2,1)S(1)} %collective-permute-done.2.f1), channel_id=1, source_target_pairs={{0,2},{2,4},{4,6},{6,8},{8,10},{10,12},{12,14},{14,0},{1,3},{3,5},... | collective-permute-start | bytes 786440 | tf_op jit(solution)/shard_map/ppermute | solution.py:500
  25.4 23.9 %collective-permute-start.8 = (bf16[1024,128]{1,0:T(8,128)(2,1)S(1)}, bf16[1024,128]{1,0:T(8,128)(2,1)S(1)}, u32[]{:S(2)}, u32[]{:S(2)}) collective-permute-start(bf16[1024,128]{1,0:T(8,128)(2,1)S(1)} %collective-permute-done.3.b1), channel_id=1, source_target_pairs={{0,14},{2,0},{4,2},{6,4},{8,6},{10,8},{12,10},{14,12},{1,15},{3,1}... | collective-permute-start | bytes 786440 | tf_op jit(solution)/shard_map/ppermute | solution.py:500
  28.0 79.4 %collective-permute-start.14 = (bf16[1024,128]{1,0:T(8,128)(2,1)S(1)}, bf16[1024,128]{1,0:T(8,128)(2,1)S(1)}, u32[]{:S(2)}, u32[]{:S(2)}) collective-permute-start(bf16[1024,128]{1,0:T(8,128)(2,1)S(1)} %collective-permute-done.4.refs_3_), channel_id=1, source_target_pairs={{0,64},{16,80},{32,96},{48,112},{64,128},{80,144},{96,160},{112,17... | collective-permute-start | bytes 786440 | tf_op jit(solution)/shard_map/ppermute | solution.py:496
  49.3 58.1 %copy-start.26 = (bf16[1024,128]{1,0:T(8,128)(2,1)}, bf16[1024,128]{1,0:T(8,128)(2,1)S(1)}, u32[]{:S(2)}) copy-start(bf16[1024,128]{1,0:T(8,128)(2,1)S(1)} %collective-permute-done.9.refs_2_) | copy-start | bytes 786436
  49.3 58.1 %copy-start.27 = (bf16[1024,128]{1,0:T(8,128)(2,1)}, bf16[1024,128]{1,0:T(8,128)(2,1)S(1)}, u32[]{:S(2)}) copy-start(bf16[1024,128]{1,0:T(8,128)(2,1)S(1)} %collective-permute-done.10.refs_3_) | copy-start | bytes 786436
  49.3 58.2 %copy-start.2 = (bf16[1024,128]{1,0:T(8,128)(2,1)S(1)}, bf16[1024,128]{1,0:T(8,128)(2,1)}, u32[]{:S(2)}) copy-start(bf16[1024,128]{1,0:T(8,128)(2,1)} %copy-done.1) | copy-start | bytes 786436
  49.3 58.2 %copy-start.4 = (s32[6]{0:T(128)S(1)}, s32[6]{0:T(128)}, u32[]{:S(2)}) copy-start(s32[6]{0:T(128)} %stack.27.meta) | copy-start | bytes 76
  49.3 58.2 %copy-start.6 = (bf16[4,16,4096]{2,1,0:T(8,128)(2,1)S(1)}, bf16[4,16,4096]{2,1,0:T(8,128)(2,1)}, u32[]{:S(2)}) copy-start(bf16[4,16,4096]{2,1,0:T(8,128)(2,1)} %q_ref.1) | copy-start | bytes 1572868
  49.3 58.2 %copy-start.7 = (bf16[4,16,256]{2,1,0:T(8,128)(2,1)S(1)}, bf16[4,16,256]{2,1,0:T(8,128)(2,1)}, u32[]{:S(2)}) copy-start(bf16[4,16,256]{2,1,0:T(8,128)(2,1)} %nk_ref.1) | copy-start | bytes 98308
  49.4 58.2 %copy-start.8 = (bf16[4,16,256]{2,1,0:T(8,128)(2,1)S(1)}, bf16[4,16,256]{2,1,0:T(8,128)(2,1)}, u32[]{:S(2)}) copy-start(bf16[4,16,256]{2,1,0:T(8,128)(2,1)} %nv_ref.1) | copy-start | bytes 98308
  49.4 58.2 %copy-start.9 = (s32[8,32]{1,0:T(8,128)S(1)}, s32[8,32]{1,0:T(8,128)}, u32[]{:S(2)}) copy-start(s32[8,32]{1,0:T(8,128)} %table.1) | copy-start | bytes 3076
  49.4 58.1 %collective-permute-start.11 = (bf16[1024,128]{1,0:T(8,128)(2,1)S(1)}, bf16[1024,128]{1,0:T(8,128)(2,1)S(1)}, u32[]{:S(2)}, u32[]{:S(2)}) collective-permute-start(bf16[1024,128]{1,0:T(8,128)(2,1)S(1)} %collective-permute-done.7.f2), channel_id=1, source_target_pairs={{0,2},{2,4},{4,6},{6,8},{8,10},{10,12},{12,14},{14,0},{1,3},{3,5},... | collective-permute-start | bytes 786440 | tf_op jit(solution)/shard_map/ppermute | solution.py:500
  49.5 58.0 %collective-permute-start.13 = (bf16[1024,128]{1,0:T(8,128)(2,1)S(1)}, bf16[1024,128]{1,0:T(8,128)(2,1)S(1)}, u32[]{:S(2)}, u32[]{:S(2)}) collective-permute-start(bf16[1024,128]{1,0:T(8,128)(2,1)S(1)} %collective-permute-done.7.f2), channel_id=1, source_target_pairs={{0,4},{2,6},{4,8},{6,10},{8,12},{10,14},{12,0},{14,2},{1,5},{3,7},... | collective-permute-start | bytes 786440 | tf_op jit(solution)/shard_map/ppermute | solution.py:500
  51.0 56.5 %collective-permute-start.12 = (bf16[1024,128]{1,0:T(8,128)(2,1)S(1)}, bf16[1024,128]{1,0:T(8,128)(2,1)S(1)}, u32[]{:S(2)}, u32[]{:S(2)}) collective-permute-start(bf16[1024,128]{1,0:T(8,128)(2,1)S(1)} %collective-permute-done.8.b2), channel_id=1, source_target_pairs={{0,14},{2,0},{4,2},{6,4},{8,6},{10,8},{12,10},{14,12},{1,15},{3,1}... | collective-permute-start | bytes 786440 | tf_op jit(solution)/shard_map/ppermute | solution.py:500
  52.1 55.3 %collective-permute-start.15 = (bf16[1024,128]{1,0:T(8,128)(2,1)S(1)}, bf16[1024,128]{1,0:T(8,128)(2,1)S(1)}, u32[]{:S(2)}, u32[]{:S(2)}) collective-permute-start(bf16[1024,128]{1,0:T(8,128)(2,1)S(1)} %collective-permute-done.10.refs_3_), channel_id=1, source_target_pairs={{0,192},{16,208},{32,224},{48,240},{64,0},{80,16},{96,32},{112,48}... | collective-permute-start | bytes 786440 | tf_op jit(solution)/shard_map/ppermute | solution.py:496
  107.4 3.1 copy-start.28
  107.5 3.1 copy-start.29
  110.6 0.6 copy-start.3
  111.2 239.4 %copy-start.5 = (s32[6]{0:T(128)S(1)}, s32[6]{0:T(128)}, u32[]{:S(2)}) copy-start(s32[6]{0:T(128)} %stack.27.meta) | copy-start | bytes 76
  111.2 45.8 %collective-permute-start.16 = (bf16[64,1152]{1,0:T(8,128)(2,1)S(1)}, bf16[64,1152]{1,0:T(8,128)(2,1)S(1)}, u32[]{:S(2)}, u32[]{:S(2)}) collective-permute-start(bf16[64,1152]{1,0:T(8,128)(2,1)S(1)} %get-tuple-element.63), channel_id=1, source_target_pairs={{0,32},{16,48},{32,0},{48,16},{64,96},{80,112},{96,64},{112,80},{1... | collective-permute-start | bytes 442376 | tf_op jit(solution)/shard_map/ppermute | solution.py:496
  157.0 5.0 %copy-start.11 = (bf16[64,1152]{1,0:T(8,128)(2,1)}, bf16[64,1152]{1,0:T(8,128)(2,1)S(1)}, u32[]{:S(2)}) copy-start(bf16[64,1152]{1,0:T(8,128)(2,1)S(1)} %collective-permute-done.16.refs_1_) | copy-start | bytes 442372
  157.0 187.3 %collective-permute-start.20 = (bf16[256,2048]{1,0:T(8,128)(2,1)}, bf16[256,2048]{1,0:T(8,128)(2,1)S(1)}, u32[]{:S(2)}, u32[]{:S(2)}) collective-permute-start(bf16[256,2048]{1,0:T(8,128)(2,1)} %get-tuple-element.78), channel_id=1, source_target_pairs={{0,16},{16,0},{32,48},{48,32},{64,80},{80,64},{96,112},{112,96},{1... | collective-permute-start | bytes 3145736 | tf_op jit(solution)/shard_map/ppermute | solution.py:496
  163.9 176.1 %collective-permute-start.17 = (bf16[64,384]{1,0:T(8,128)(2,1)}, bf16[64,384]{1,0:T(8,128)(2,1)S(1)}, u32[]{:S(2)}, u32[]{:S(2)}) collective-permute-start(bf16[64,384]{1,0:T(8,128)(2,1)} %get-tuple-element.75), channel_id=1, source_target_pairs={{0,64},{16,80},{32,96},{48,112},{64,0},{80,16},{96,32},{112,48},{1... | collective-permute-start | bytes 147464 | tf_op jit(solution)/shard_map/ppermute | solution.py:496
  197.8 144.6 %collective-permute-start.18 = (bf16[64,384]{1,0:T(8,128)(2,1)}, bf16[64,384]{1,0:T(8,128)(2,1)S(1)}, u32[]{:S(2)}, u32[]{:S(2)}) collective-permute-start(bf16[64,384]{1,0:T(8,128)(2,1)} %get-tuple-element.76), channel_id=1, source_target_pairs={{0,128},{16,144},{32,160},{48,176},{64,192},{80,208},{96,224},{112... | collective-permute-start | bytes 147464 | tf_op jit(solution)/shard_map/ppermute | solution.py:496
  340.0 4.4 %collective-permute-start.19 = (bf16[64,384]{1,0:T(8,128)(2,1)}, bf16[64,384]{1,0:T(8,128)(2,1)S(1)}, u32[]{:S(2)}, u32[]{:S(2)}) collective-permute-start(bf16[64,384]{1,0:T(8,128)(2,1)} %get-tuple-element.77), channel_id=1, source_target_pairs={{0,192},{16,208},{32,224},{48,240},{64,128},{80,144},{96,160},{112... | collective-permute-start | bytes 147464 | tf_op jit(solution)/shard_map/ppermute | solution.py:496
  340.0 4.4 %copy-start.18 = (bf16[64,384]{1,0:T(8,128)(2,1)}, bf16[64,384]{1,0:T(8,128)(2,1)S(1)}, u32[]{:S(2)}) copy-start(bf16[64,384]{1,0:T(8,128)(2,1)S(1)} %collective-permute-done.17.refs_1_) | copy-start | bytes 147460
  342.5 1.9 copy-start.19
  344.3 0.6 copy-start.20
  346.7 7.0 %collective-permute-start.21 = (bf16[64,256]{1,0:T(8,128)(2,1)}, bf16[64,256]{1,0:T(8,128)(2,1)S(1)}, u32[]{:S(2)}, u32[]{:S(2)}) collective-permute-start(bf16[64,256]{1,0:T(8,128)(2,1)} %merge.3), channel_id=1, source_target_pairs={{0,64},{16,80},{32,96},{48,112},{64,0},{80,16},{96,32},{112,48},{1... | collective-permute-start | bytes 98312 | tf_op jit(solution)/shard_map/ppermute | solution.py:496
  346.7 7.0 %collective-permute-start.22 = (bf16[64,256]{1,0:T(8,128)(2,1)}, bf16[64,256]{1,0:T(8,128)(2,1)S(1)}, u32[]{:S(2)}, u32[]{:S(2)}) collective-permute-start(bf16[64,256]{1,0:T(8,128)(2,1)} %merge.3), channel_id=1, source_target_pairs={{0,128},{16,144},{32,160},{48,176},{64,192},{80,208},{96,224},{112... | collective-permute-start | bytes 98312 | tf_op jit(solution)/shard_map/ppermute | solution.py:496
  348.4 5.4 %collective-permute-start.23 = (bf16[64,256]{1,0:T(8,128)(2,1)}, bf16[64,256]{1,0:T(8,128)(2,1)S(1)}, u32[]{:S(2)}, u32[]{:S(2)}) collective-permute-start(bf16[64,256]{1,0:T(8,128)(2,1)} %merge.3), channel_id=1, source_target_pairs={{0,192},{16,208},{32,224},{48,240},{64,128},{80,144},{96,160},{112... | collective-permute-start | bytes 98312 | tf_op jit(solution)/shard_map/ppermute | solution.py:496
  350.6 1.2 copy-start
  351.8 1.9 copy-start.14
  353.8 11.4 %copy-start.10 = (bf16[64,1024]{1,0:T(8,128)(2,1)}, bf16[64,1024]{1,0:T(8,128)(2,1)S(1)}, u32[]{:S(2)}) copy-start(bf16[64,1024]{1,0:T(8,128)(2,1)S(1)} %pad_maximum_fusion.3) | copy-start | bytes 393220
  353.8 6.1 %collective-permute-start.24 = (bf16[64,1024]{1,0:T(8,128)(2,1)S(1)}, bf16[64,1024]{1,0:T(8,128)(2,1)S(1)}, u32[]{:S(2)}, u32[]{:S(2)}) collective-permute-start(bf16[64,1024]{1,0:T(8,128)(2,1)S(1)} %pad_maximum_fusion.3), channel_id=1, source_target_pairs={{0,32},{16,48},{32,0},{48,16},{64,96},{80,112},{96,64},{112,80},{1... | collective-permute-start | bytes 393224 | tf_op jit(solution)/shard_map/ppermute | solution.py:496
  353.9 6.0 %collective-permute-start.25 = (bf16[64,1024]{1,0:T(8,128)(2,1)S(1)}, bf16[64,1024]{1,0:T(8,128)(2,1)S(1)}, u32[]{:S(2)}, u32[]{:S(2)}) collective-permute-start(bf16[64,1024]{1,0:T(8,128)(2,1)S(1)} %pad_maximum_fusion.3), channel_id=1, source_target_pairs={{0,16},{16,0},{32,48},{48,32},{64,80},{80,64},{96,112},{112,96},{1... | collective-permute-start | bytes 393224 | tf_op jit(solution)/shard_map/ppermute | solution.py:496
  356.9 8.3 %collective-permute-start.26 = (bf16[64,1024]{1,0:T(8,128)(2,1)S(1)}, bf16[64,1024]{1,0:T(8,128)(2,1)S(1)}, u32[]{:S(2)}, u32[]{:S(2)}) collective-permute-start(bf16[64,1024]{1,0:T(8,128)(2,1)S(1)} %pad_maximum_fusion.3), channel_id=1, source_target_pairs={{0,48},{16,32},{32,16},{48,0},{64,112},{80,96},{96,80},{112,64},{1... | collective-permute-start | bytes 393224 | tf_op jit(solution)/shard_map/ppermute | solution.py:496
  359.9 5.3 %copy-start.15 = (bf16[64,1024]{1,0:T(8,128)(2,1)}, bf16[64,1024]{1,0:T(8,128)(2,1)S(1)}, u32[]{:S(2)}) copy-start(bf16[64,1024]{1,0:T(8,128)(2,1)S(1)} %collective-permute-done.24) | copy-start | bytes 393220
  359.9 5.3 %copy-start.16 = (bf16[64,1024]{1,0:T(8,128)(2,1)}, bf16[64,1024]{1,0:T(8,128)(2,1)S(1)}, u32[]{:S(2)}) copy-start(bf16[64,1024]{1,0:T(8,128)(2,1)S(1)} %collective-permute-done.25) | copy-start | bytes 393220
  365.2 0.7 copy-start.17
where the time goes:
time: 375 us; the launch traced here: 368 us
  starting transfers between devices  281 us (75%)
  Pallas kernels  64.2 us (17%)
  waiting for transfers between devices  16.4 us (4%)
  local copies, waits for them, and re-layouts  5.31 us (1%)
    ppermute x20, starting transfers between devices, ctx_move(): return lax.ppermute(array, 'ctx', pairs)  271 us
    pallas_call x3, Pallas kernels, prefill(): pl.pallas_call(functools.partial(prefill_kernel, group=group, rows=rows,...  53.6 us
    ppermute x20, waiting for transfers between devices, ctx_move(): return lax.ppermute(array, 'ctx', pairs)  16.3 us
    ppermute x7, starting transfers between devices, dec_move(): return lax.ppermute(array, 'dec', [(i, (i + dz) % 8) for i in range(8)])  9.42 us
  transfers between devices with their start and end apart: 27, of which 6 were waited for; matrix products, arithmetic and copies ran while one was open for 0% of the time, Pallas kernels for 16%

commit v1 on v0

--- a/solution.py
+++ b/solution.py
@@ -181,38 +181,49 @@
     def _online():
         sums = state if first else acc
         lane = lax.broadcasted_iota(jnp.int32, (rows, 2 * HD), 1)
-        for g, side, r, at, q in tiles():
-            if first:
-                sums[g, at, :] = jnp.zeros((rows, 2 * HD), F32)
-                best0 = jnp.full((rows, 1), NEG, F32)
-            else:
-                old = started(g, at)
-                sums[g, at, :] = jnp.where(lane >= HD, old[:, HD : HD + 1], old)
-                best0 = jnp.where(shifted, old[:, 2 * HD - 1 :], 0.0)
-            own_ok = allowed(side, r) if first else None
-
-            def one(index, best, q=q, g=g, at=at, own_ok=own_ok):
-                base = pl.multiple_of(index * 512, 512)
-                s = dot_nt(q, ks[pl.ds(base, 512), :]) * SCALE
-                if own_ok is not None:
-                    s = jnp.where(jnp.logical_or(own_ok, index > 0), s, NEG)
-                new = jnp.maximum(best, jnp.max(s, axis=1, keepdims=True))
-                p = jnp.exp(s - new)
-                if own_ok is not None:
-                    p = jnp.where(jnp.logical_or(own_ok, index > 0), p, 0.0)
-                sums[g, at, :] = sums[g, at, :] * jnp.exp(best - new) + dot_nn(
-                    p.astype(BF16), vx[pl.ds(base, 512), :]
-                )
-                return new
-
-            best = lax.fori_loop(0, count, one, best0)
-            if first:
-                sums[g, at, :] = jnp.where(lane == 2 * HD - 1, best, sums[g, at, :])
-            else:
-                write(g, side, at, sums[g, at, :])
-
-
-def prefill(meta, queries, q_oth, bufs, head, heads, before=None, group=4, rows=128):
+        for side in range(2):
+
+            def tile(number, carry, side=side):
+                g, r = number // (half // rows), lax.rem(number, half // rows)
+                q = q_refs[side][pl.ds(pl.multiple_of(r * rows, rows), rows), pl.ds(pl.multiple_of(g * HD, HD), HD)]
+                at = pl.ds(pl.multiple_of(side * half + r * rows, rows), rows)
+                if first:
+                    sums[g, at, :] = jnp.zeros((rows, 2 * HD), F32)
+                    best0 = jnp.full((rows, 1), NEG, F32)
+                else:
+                    old = started(g, at)
+                    sums[g, at, :] = jnp.where(lane >= HD, old[:, HD : HD + 1], old)
+                    best0 = jnp.where(shifted, old[:, 2 * HD - 1 :], 0.0)
+                own_ok = allowed(side, r) if first else None
+
+                def one(index, best):
+                    base = pl.multiple_of(index * 512, 512)
+                    s = dot_nt(q, ks[pl.ds(base, 512), :]) * SCALE
+                    if own_ok is not None:
+                        s = jnp.where(jnp.logical_or(own_ok, index > 0), s, NEG)
+                    new = jnp.maximum(best, jnp.max(s, axis=1, keepdims=True))
+                    p = jnp.exp(s - new)
+                    if own_ok is not None:
+                        p = jnp.where(jnp.logical_or(own_ok, index > 0), p, 0.0)
+                    sums[g, at, :] = sums[g, at, :] * jnp.exp(best - new) + dot_nn(
+                        p.astype(BF16), vx[pl.ds(base, 512), :]
+                    )
+                    return new
+
+                best = lax.fori_loop(0, count, one, best0)
+                both = sums[g, at, :]
+                if first:
+                    sums[g, at, :] = jnp.where(lane == 2 * HD - 1, best, both)
+                else:
+                    (o_own, o_oth)[side][
+                        pl.ds(pl.multiple_of(r * rows, rows), rows), pl.ds(pl.multiple_of(g * HD, HD), HD)
+                    ] = (both[:, :HD] / both[:, HD:]).astype(BF16)
+                return carry
+
+            lax.fori_loop(0, group * (half // rows), tile, 0)
+
+
+def prefill(meta, queries, q_oth, bufs, head, heads, before=None, group=2, rows=128):
     per = 16 // group
     at = head // group
     first = before is None
@@ -298,12 +309,38 @@
     )(meta, *parts)
 
 
+def pick_kernel(meta, table, own, f1, b1, up, down):
+    chip, core, z = meta[0], meta[1], meta[4]
+    for out, shift in ((up, 3), (down, 5)):
+        goal = lax.rem(z + shift, 8)
+        for page in range(4):
+            side, inner = page // 2, page % 2
+            from_core = core if side == 0 else 1 - core
+            rel = lax.rem(table[goal, chip * 4 + from_core * 2 + inner] - z + 8, 8)
+            for kind in range(2):
+                off = side * 512 + kind * 256 + inner * PAGE
+                at = slice(off, off + PAGE)
+                out[at, :] = jnp.where(rel == 1, b1[at, :], jnp.where(rel == 7, f1[at, :], own[at, :]))
+
+
+def pick(meta, table, own, f1, b1):
+    smem = pl.BlockSpec(memory_space=pltpu.SMEM)
+    vmem = pl.BlockSpec(memory_space=pltpu.VMEM)
+    return pl.pallas_call(
+        pick_kernel,
+        in_specs=[smem, smem, vmem, vmem, vmem],
+        out_specs=[vmem, vmem],
+        out_shape=[jax.ShapeDtypeStruct((1024, HD), BF16)] * 2,
+        name="pick",
+    )(meta, table, own, f1, b1)
+
+
 def decode_kernel(
-    meta, table, q_ref, nk_ref, nv_ref, len_ref, own, f1, f2, f3, f4, b1, b2, b3,
+    meta, table, q_ref, nk_ref, nv_ref, len_ref, own, f1, b1, fs, bs,
     keep, send, ks, vx, sem,
 ):
     chip, core, zpos, mask = meta[0], meta[1], meta[4], meta[5]
-    sources = {0: own, 7: f1, 6: f2, 5: f3, 4: f4, 1: b1, 2: b2, 3: b3}
+    sources = {0: own, 7: f1, 1: b1, 2: bs, 3: bs, 4: fs, 5: fs, 6: fs}
 
     def page_copy(buf, off, page):
         return (
@@ -387,7 +424,7 @@
                 pl.BlockSpec((4, 16, HD), lambda i, m, t: (0, 0, m[1])),
                 pl.BlockSpec((64, 1), lambda i, m, t: (0, 0)),
             ]
-            + [any_spec] * 8,
+            + [any_spec] * 5,
             out_specs=[pl.BlockSpec((64, 9 * HD), lambda i, m, t: (0, 0))] * 2,
             scratch_shapes=[
                 pltpu.VMEM((512 + 64, HD), BF16),
@@ -402,8 +439,13 @@
     )(meta, table, dec_q, dec_k, dec_v, lens, *bufs)
 
 
-def merge_kernel(*refs, count, heads, last):
-    ins, outs = refs[:count], refs[count:]
+def merge_kernel(meta, *refs, count, heads, last):
+    ins, out = refs[:count], refs[count]
+    if last:
+        held = refs[count + 1]
+        for b in range(count):
+            held[meta[2] ^ b] = ins[b][...]
+        ins = [held.at[k] for k in range(count)]
     cols = heads * HD
     lane = lax.broadcasted_iota(jnp.int32, (64, HD), 1)
     stats_in = [ref[:, cols:].astype(F32) for ref in ins]
@@ -430,31 +472,29 @@
         return dot_nn(high, place) + dot_nn(low, place)
 
     joined = sum(ref[:, :cols].astype(F32) * spread(w) for ref, w in zip(ins, shares))
+    out[:, :cols] = joined.astype(BF16)
     if last:
-        outs[0][...] = joined.astype(BF16)
         return
     high = total.astype(BF16).astype(F32)
-    low = total - high
-    each = heads // len(outs)
-    for part, out in enumerate(outs):
-        first = part * each
-        out[:, : each * HD] = joined[:, first * HD : (first + each) * HD].astype(BF16)
-        stats = jnp.zeros((64, HD), F32)
-        for values, goal in ((best, 0), (high, 16), (low, 32)):
-            turn = (goal - first) % HD
-            moved = pltpu.roll(values, turn, 1) if turn else values
-            stats = jnp.where((lane >= goal) & (lane < goal + each), moved, stats)
-        out[:, each * HD :] = stats.astype(BF16)
-
-
-def merge(parts, heads, runs, last=False):
-    width = heads * HD if last else (heads // runs + 1) * HD
+    stats = jnp.zeros((64, HD), F32)
+    for values, goal in ((best, 0), (high, 16), (total - high, 32)):
+        moved = pltpu.roll(values, goal, 1) if goal else values
+        stats = jnp.where((lane >= goal) & (lane < goal + heads), moved, stats)
+    out[:, cols:] = stats.astype(BF16)
+
+
+def merge(meta, parts, heads, last=False):
+    width = heads * HD if last else (heads + 1) * HD
+    vmem = pl.BlockSpec(memory_space=pltpu.VMEM)
     return pl.pallas_call(
         functools.partial(merge_kernel, count=len(parts), heads=heads, last=last),
-        out_shape=[jax.ShapeDtypeStruct((64, width), BF16)] * runs,
+        in_specs=[pl.BlockSpec(memory_space=pltpu.SMEM)] + [vmem] * len(parts),
+        out_specs=vmem,
+        scratch_shapes=[pltpu.VMEM((len(parts), 64, (heads + 1) * HD), BF16)] if last else [],
+        out_shape=jax.ShapeDtypeStruct((64, width), BF16),
         cost_estimate=pl.CostEstimate(flops=10**6, bytes_accessed=2**18, transcendentals=0),
         name="merge",
-    )(*parts)
+    )(meta, *parts)
 
 
 def place_kernel(meta, *refs):
@@ -505,7 +545,7 @@
     z = lax.axis_index("dec")
     x, y, core = c // 4, (c // 2) % 2, c % 2
     chip = c // 2
-    mask = y * 8 + x * 2
+    mask = y * 8
     meta = jnp.stack([chip, core, x, y, z, mask]).astype(jnp.int32)
 
     k0, v0 = keys[0], values[0]
@@ -513,46 +553,42 @@
     second = jnp.concatenate([k0[:, HD:], v0[:, HD:]], axis=0)
     mine = jnp.where(core == 0, first, second)
     other = jnp.where(core == 0, second, first)
-    q_send = lax.dynamic_slice_in_dim(queries[0], (1 - core) * 2048, 2048, 1)
     barrier = lax.optimization_barrier
-    got, q_oth = barrier((ctx_move(other, flip_core=1), ctx_move(q_send, flip_core=1)))
+    q, other = barrier((queries[0], other))
+    got = ctx_move(other, flip_core=1)
+    q_oth = ctx_move(lax.dynamic_slice_in_dim(q, (1 - core) * 2048, 2048, 1), flip_core=1)
+    got, q_oth, meta = barrier((got, q_oth, meta))
     chunk = jnp.concatenate([mine, got], axis=0)
     lens = jnp.tile(ctx_lengths, 4)[:, None]
-
-    q = queries[0]
     f1, b1 = dec_move(chunk, 1), dec_move(chunk, -1)
     rr, ll, yy = ctx_move(chunk, dx=1), ctx_move(chunk, dx=-1), ctx_move(chunk, flip_y=1)
-    f1, b1, rr, ll, yy = barrier((f1, b1, rr, ll, yy))
+    f1, b1, rr, ll, yy, lens = barrier((f1, b1, rr, ll, yy, lens))
     near = (chunk, rr, ll, yy)
-    f2, b2 = dec_move(f1, 1), dec_move(b1, -1)
-    ry, ly = ctx_move(yy, dx=1), ctx_move(yy, dx=-1)
+    up, down = pick(meta, page_table, chunk, f1, b1)
+    fs, bs = dec_move(up, 3), dec_move(down, -3)
+    ry, ly, xx = ctx_move(yy, dx=1), ctx_move(yy, dx=-1), ctx_move(rr, dx=1)
     pa0 = prefill(meta, q, q_oth, near, 0, 8)
-    f2, b2, ry, ly, pa0 = barrier((f2, b2, ry, ly, pa0))
-    f3, b3, f4 = dec_move(f2, 1), dec_move(b2, -1), dec_move(f2, 2)
-    xx, xy = ctx_move(rr, dx=1), ctx_move(ly, dx=-1)
+    ry, ly, xx, fs, bs, pa0 = barrier((ry, ly, xx, fs, bs, pa0))
+    keep, send = decode_part(
+        meta, page_table, dec_queries, dec_keys, dec_values, lens, (chunk, f1, b1, fs, bs)
+    )
+    send, meta = barrier((send, meta))
+    got = ctx_move(send, flip_y=1)
+    xy = ctx_move(ly, dx=-1)
     pa1 = prefill(meta, q, q_oth, near, 8, 8)
-    f3, b3, f4, xx, xy, pa1 = barrier((f3, b3, f4, xx, xy, pa1))
-    far = (ry, ly, xx, xy)
-
-    keep, send = decode_part(
-        meta, page_table, dec_queries, dec_keys, dec_values, lens, (chunk, f1, f2, f3, f4, b1, b2, b3)
-    )
-    got = ctx_move(send, flip_y=1)
-    own_out, oth_out = prefill(meta, q, q_oth, far, 0, 16, (pa0, pa1))
+    got, xy, pa1 = barrier((got, xy, pa1))
+    part = merge(meta, (keep, got), 8)
+    part, meta = barrier((part, meta))
+    got = [ctx_move(part, mirror_x=k) for k in (1, 2, 3)]
+    own_out, oth_out = prefill(meta, q, q_oth, (ry, ly, xx, xy), 0, 16, (pa0, pa1))
     got, own_out, oth_out = barrier((got, own_out, oth_out))
     back = ctx_move(oth_out, flip_core=1)
-    keep, *send = merge((keep, got), 8, 4)
-    got = [ctx_move(send[k - 1], mirror_x=k) for k in (1, 2, 3)]
-    got, back = barrier((got, back))
-    (part,) = merge((keep, *got), 2, 1, last=True)
-    got = [ctx_move(part, mirror_x=k) for k in (1, 2, 3)]
+    part = merge(meta, (part, *got), 8, last=True)
+    part, back = barrier((part, back))
+    got = [ctx_move(part, flip_y=1), ctx_move(part, flip_core=1), ctx_move(part, flip_y=1, flip_core=1)]
     prefill_out = join(meta, [own_out], [back])
     got, prefill_out = barrier((got, prefill_out))
-    part = jnp.concatenate([part, *got], axis=1)
-    decode_out = place(
-        meta,
-        [part, ctx_move(part, flip_y=1), ctx_move(part, flip_core=1), ctx_move(part, flip_y=1, flip_core=1)],
-    )
+    decode_out = place(meta, [part, *got])
     return (prefill_out[None], decode_out)
 
 

time: 375 us -> 357 us (0.952)
  the two profiles are of different devices: /device:TPU:1 before, /device:TPU:31 now
where the time goes in v1:
time: 357 us; the launch traced here: 356 us
  Pallas kernels  307 us (86%)
  starting transfers between devices  28.7 us (8%)
  waiting for transfers between devices  13 us (4%)
  local copies, waits for them, and re-layouts  6.33 us (2%)
    pallas_call x3, Pallas kernels, prefill(): pl.pallas_call(functools.partial(prefill_kernel, group=group, rows=rows,...  294 us
    ppermute x17, starting transfers between devices, ctx_move(): return lax.ppermute(array, 'ctx', pairs)  18.4 us
    ppermute x4, starting transfers between devices, dec_move(): return lax.ppermute(array, 'dec', [(i, (i + dz) % 8) for i in range(8)])  10.3 us
    ppermute x4, waiting for transfers between devices, dec_move(): return lax.ppermute(array, 'dec', [(i, (i + dz) % 8) for i in range(8)])  7.36 us
  transfers between devices with their start and end apart: 21, of which 7 were waited for; matrix products, arithmetic and copies ran while one was open for 0% of the time, Pallas kernels for 84%

profile of v1, /device:TPU:31, one launch (start us, length us, event | category | flops | bytes accessed | tf_op | source)
XLA Modules:
  0.0 356.4 jit_solution(14034834389226010423)
XLA Ops:
  0.7 1.0 fusion
  1.6 0.1 broadcast_select_fusion
  1.7 1.3 constant_dynamic-slice_fusion
  3.0 0.8 collective-permute-start.1
  3.8 0.1 collective-permute-start
  3.9 0.6 stack.27.meta
  4.5 1.7 collective-permute-done
  6.2 0.0 collective-permute-done.1.refs_1_
  6.3 0.0 copy-start.1
  6.3 1.0 collective-permute-start.6
  7.3 0.5 collective-permute-start.5
  7.9 2.1 collective-permute-start.4
  10.0 5.6 %collective-permute-start.3 = (bf16[1024,128]{1,0:T(8,128)(2,1)S(1)}, bf16[1024,128]{1,0:T(8,128)(2,1)S(1)}, u32[]{:S(2)}, u32[]{:S(2)}) collective-permute-start(bf16[1024,128]{1,0:T(8,128)(2,1)S(1)} %pad_maximum_fusion.own.refs_2_), channel_id=1, source_target_pairs={{0,14},{2,0},{4,2},{6,4},{8,6},{10,8},{12,10},{14,12},{1,15},{3,1}... | collective-permute-start | bytes 786440 | tf_op jit(solution)/shard_map/ppermute | solution.py:540
  15.6 0.0 collective-permute-start.2
  15.6 0.1 broadcast_in_dim_tile.3
  15.7 0.0 collective-permute-done.6.refs_5_
  15.7 0.1 collective-permute-done.5.refs_4_
  15.7 0.0 collective-permute-done.4.refs_3_
  15.7 4.2 %collective-permute-done.3.b1 = bf16[1024,128]{1,0:T(8,128)(2,1)S(1)} collective-permute-done((bf16[1024,128]{1,0:T(8,128)(2,1)S(1)}, bf16[1024,128]{1,0:T(8,128)(2,1)S(1)}, u32[]{:S(2)}, u32[]{:S(2)}) %collective-permute-start.3) | collective-permute-done | bytes 262176 | tf_op jit(solution)/shard_map/ppermute | solution.py:540
  19.9 3.1 collective-permute-done.2.f1
  23.1 0.0 collective-permute-start.8
  23.1 2.7 collective-permute-start.7
  25.8 0.0 collective-permute-start.9
  25.8 2.1 pick.1
  27.9 0.0 collective-permute-start.10
  28.0 0.0 copy-start.10
  28.0 0.0 copy-start.11
  28.0 0.0 copy-start.12
  28.0 0.0 copy-start.13
  28.0 4.7 %collective-permute-start.11 = (bf16[1024,128]{1,0:T(8,128)(2,1)}, bf16[1024,128]{1,0:T(8,128)(2,1)S(1)}, u32[]{:S(2)}, u32[]{:S(2)}) collective-permute-start(bf16[1024,128]{1,0:T(8,128)(2,1)} %get-tuple-element.59), channel_id=1, source_target_pairs={{0,10},{2,12},{4,14},{6,0},{8,2},{10,4},{12,6},{14,8},{1,11},{3,13... | collective-permute-start | bytes 786440 | tf_op jit(solution)/shard_map/ppermute | solution.py:540
  32.7 68.4 %prefill_a.2 = (f32[8,512,256]{2,1,0:T(8,128)}, s32[4]{0:T(128)}) custom-call(s32[6]{0:T(128)} %stack.27.meta, bf16[256,4096]{1,0:T(8,128)(2,1)} %bitcast.16, bf16[256,2048]{1,0:T(8,128)(2,1)} %copy-done.22, bf16[1024,128]{1,0:T(8,128)(2,1)} %copy-done.1, bf16[1024,128]{1,0:T(8,128)(2,1)} %collective-permute-done.4.refs_3_, bf16[1024,128]{1,0:T(8,128)(2,1)} %copy-done.24, ...), custom_call_target="tpu_custom_call" | custom-call | flops 8589934592 | bytes 4194304 | tf_op jit(solution)/shard_map/prefill_a/pallas_call | solution.py:260
  101.2 0.1 copy.10.len_ref
  101.3 0.0 collective-permute-done.9.refs_4_
  101.3 0.0 collective-permute-done.8.refs_3_
  101.3 0.0 collective-permute-done.7.refs_2_
  101.3 0.0 collective-permute-done.10.fs
  101.3 0.0 collective-permute-done.11.bs
  101.4 2.8 decode_part.1
  104.3 0.6 copy-done.7
  104.9 0.0 collective-permute-start.12
  104.9 0.0 collective-permute-start.13
  104.9 68.5 %prefill_a.3 = (f32[8,512,256]{2,1,0:T(8,128)}, s32[4]{0:T(128)}) custom-call(s32[6]{0:T(128)} %stack.27.meta, bf16[256,4096]{1,0:T(8,128)(2,1)} %bitcast.17, bf16[256,2048]{1,0:T(8,128)(2,1)} %copy-done.22, bf16[1024,128]{1,0:T(8,128)(2,1)} %copy-done.1, bf16[1024,128]{1,0:T(8,128)(2,1)} %collective-permute-done.4.refs_3_, bf16[1024,128]{1,0:T(8,128)(2,1)} %copy-done.24, ...), custom_call_target="tpu_custom_call" | custom-call | flops 8589934592 | bytes 4194304 | tf_op jit(solution)/shard_map/prefill_a/pallas_call | solution.py:260
  173.4 0.0 collective-permute-done.13.refs_5_
  173.4 0.0 copy-start.25
  173.4 0.6 copy-done.17
  174.1 1.9 merge.2.refs_0_
  176.0 0.0 collective-permute-start.16
  176.0 0.0 collective-permute-start.15
  176.0 3.2 collective-permute-start.14
  179.3 157.0 %prefill_b.1 = (bf16[256,2048]{1,0:T(8,128)(2,1)}, bf16[256,2048]{1,0:T(8,128)(2,1)}) custom-call(s32[6]{0:T(128)} %stack.27.meta, bf16[256,4096]{1,0:T(8,128)(2,1)} %bitcast.18, bf16[256,2048]{1,0:T(8,128)(2,1)} %copy-done.22, bf16[1024,128]{1,0:T(8,128)(2,1)} %collective-permute-done.7.refs_2_, bf16[1024,128]{1,0:T(8,128)(2,1)} %collective-permute-done.8.refs_3_, ...), custom_call_target="tpu_custom_call" | custom-call | flops 17179869184 | bytes 4194304 | tf_op jit(solution)/shard_map/prefill_b/pallas_call | solution.py:260
  336.3 0.0 collective-permute-done.15.refs_2_
  336.4 0.0 copy-start.15
  336.4 0.0 copy-start.16
  336.4 4.5 %collective-permute-start.17 = (bf16[256,2048]{1,0:T(8,128)(2,1)}, bf16[256,2048]{1,0:T(8,128)(2,1)S(1)}, u32[]{:S(2)}, u32[]{:S(2)}) collective-permute-start(bf16[256,2048]{1,0:T(8,128)(2,1)} %get-tuple-element.88), channel_id=1, source_target_pairs={{0,16},{16,0},{32,48},{48,32},{64,80},{80,64},{96,112},{112,96},{1... | collective-permute-start | bytes 3145736 | tf_op jit(solution)/shard_map/ppermute | solution.py:536
  340.9 2.3 merge.3
  343.2 0.1 collective-permute-done.17.refs_1_
  343.4 0.6 collective-permute-start.19
  343.9 2.8 collective-permute-start.18
  346.7 1.2 copy-done
  348.0 1.9 join.1
  349.8 1.0 collective-permute-done.20
  350.9 2.6 collective-permute-done.18
  353.5 0.6 copy-done.20
  354.2 2.0 place.1
  (47 shorter events, 0.1 us)
Async XLA Ops:
  0.6 14.9 %copy-start.21 = (s32[16]{0:T(128)S(1)}, s32[16]{0:T(128)}, u32[]{:S(2)}) copy-start(s32[16]{0:T(128)} %param.15) | copy-start | bytes 196
  3.0 3.2 collective-permute-start.1
  3.8 2.5 collective-permute-start
  6.2 26.5 %copy-start.22 = (bf16[256,2048]{1,0:T(8,128)(2,1)}, bf16[256,2048]{1,0:T(8,128)(2,1)S(1)}, u32[]{:S(2)}) copy-start(bf16[256,2048]{1,0:T(8,128)(2,1)S(1)} %collective-permute-done.1.refs_1_) | copy-start | bytes 3145732
  6.3 19.5 %copy-start.1 = (bf16[1024,128]{1,0:T(8,128)(2,1)}, bf16[1024,128]{1,0:T(8,128)(2,1)S(1)}, u32[]{:S(2)}) copy-start(bf16[1024,128]{1,0:T(8,128)(2,1)S(1)} %pad_maximum_fusion.own.refs_2_) | copy-start | bytes 786436
  6.3 9.4 %collective-permute-start.6 = (bf16[1024,128]{1,0:T(8,128)(2,1)S(1)}, bf16[1024,128]{1,0:T(8,128)(2,1)S(1)}, u32[]{:S(2)}, u32[]{:S(2)}) collective-permute-start(bf16[1024,128]{1,0:T(8,128)(2,1)S(1)} %pad_maximum_fusion.own.refs_2_), channel_id=1, source_target_pairs={{0,32},{16,48},{32,0},{48,16},{64,96},{80,112},{96,64},{112,80},{1... | collective-permute-start | bytes 786440 | tf_op jit(solution)/shard_map/ppermute | solution.py:536
  7.3 8.4 %collective-permute-start.5 = (bf16[1024,128]{1,0:T(8,128)(2,1)S(1)}, bf16[1024,128]{1,0:T(8,128)(2,1)S(1)}, u32[]{:S(2)}, u32[]{:S(2)}) collective-permute-start(bf16[1024,128]{1,0:T(8,128)(2,1)S(1)} %pad_maximum_fusion.own.refs_2_), channel_id=1, source_target_pairs={{0,192},{16,208},{32,224},{48,240},{64,0},{80,16},{96,32},{112,48}... | collective-permute-start | bytes 786440 | tf_op jit(solution)/shard_map/ppermute | solution.py:536
  7.9 7.9 %collective-permute-start.4 = (bf16[1024,128]{1,0:T(8,128)(2,1)S(1)}, bf16[1024,128]{1,0:T(8,128)(2,1)}, u32[]{:S(2)}, u32[]{:S(2)}) collective-permute-start(bf16[1024,128]{1,0:T(8,128)(2,1)S(1)} %pad_maximum_fusion.own.refs_2_), channel_id=1, source_target_pairs={{0,64},{16,80},{32,96},{48,112},{64,128},{80,144},{96,160},{112,17... | collective-permute-start | bytes 786440 | tf_op jit(solution)/shard_map/ppermute | solution.py:536
  10.0 10.0 %collective-permute-start.3 = (bf16[1024,128]{1,0:T(8,128)(2,1)S(1)}, bf16[1024,128]{1,0:T(8,128)(2,1)S(1)}, u32[]{:S(2)}, u32[]{:S(2)}) collective-permute-start(bf16[1024,128]{1,0:T(8,128)(2,1)S(1)} %pad_maximum_fusion.own.refs_2_), channel_id=1, source_target_pairs={{0,14},{2,0},{4,2},{6,4},{8,6},{10,8},{12,10},{14,12},{1,15},{3,1}... | collective-permute-start | bytes 786440 | tf_op jit(solution)/shard_map/ppermute | solution.py:540
  15.6 7.5 %collective-permute-start.2 = (bf16[1024,128]{1,0:T(8,128)(2,1)S(1)}, bf16[1024,128]{1,0:T(8,128)(2,1)S(1)}, u32[]{:S(2)}, u32[]{:S(2)}) collective-permute-start(bf16[1024,128]{1,0:T(8,128)(2,1)S(1)} %pad_maximum_fusion.own.refs_2_), channel_id=1, source_target_pairs={{0,2},{2,4},{4,6},{6,8},{8,10},{10,12},{12,14},{14,0},{1,3},{3,5},... | collective-permute-start | bytes 786440 | tf_op jit(solution)/shard_map/ppermute | solution.py:540
  15.7 17.1 %copy-start.23 = (bf16[1024,128]{1,0:T(8,128)(2,1)}, bf16[1024,128]{1,0:T(8,128)(2,1)S(1)}, u32[]{:S(2)}) copy-start(bf16[1024,128]{1,0:T(8,128)(2,1)S(1)} %collective-permute-done.6.refs_5_) | copy-start | bytes 786436
  15.7 17.0 %copy-start.24 = (bf16[1024,128]{1,0:T(8,128)(2,1)}, bf16[1024,128]{1,0:T(8,128)(2,1)S(1)}, u32[]{:S(2)}) copy-start(bf16[1024,128]{1,0:T(8,128)(2,1)S(1)} %collective-permute-done.5.refs_4_) | copy-start | bytes 786436
  19.9 5.8 %copy-start.3 = (bf16[1024,128]{1,0:T(8,128)(2,1)}, bf16[1024,128]{1,0:T(8,128)(2,1)S(1)}, u32[]{:S(2)}) copy-start(bf16[1024,128]{1,0:T(8,128)(2,1)S(1)} %collective-permute-done.3.b1) | copy-start | bytes 786436
  23.1 2.7 copy-start.5
  23.1 78.2 %collective-permute-start.8 = (bf16[1024,128]{1,0:T(8,128)(2,1)S(1)}, bf16[1024,128]{1,0:T(8,128)(2,1)}, u32[]{:S(2)}, u32[]{:S(2)}) collective-permute-start(bf16[1024,128]{1,0:T(8,128)(2,1)S(1)} %collective-permute-done.6.refs_5_), channel_id=1, source_target_pairs={{0,192},{16,208},{32,224},{48,240},{64,0},{80,16},{96,32},{112,48}... | collective-permute-start | bytes 786440 | tf_op jit(solution)/shard_map/ppermute | solution.py:536
  23.1 78.2 %collective-permute-start.7 = (bf16[1024,128]{1,0:T(8,128)(2,1)S(1)}, bf16[1024,128]{1,0:T(8,128)(2,1)}, u32[]{:S(2)}, u32[]{:S(2)}) collective-permute-start(bf16[1024,128]{1,0:T(8,128)(2,1)S(1)} %collective-permute-done.6.refs_5_), channel_id=1, source_target_pairs={{0,64},{16,80},{32,96},{48,112},{64,128},{80,144},{96,160},{112,17... | collective-permute-start | bytes 786440 | tf_op jit(solution)/shard_map/ppermute | solution.py:536
  25.8 75.5 %collective-permute-start.9 = (bf16[1024,128]{1,0:T(8,128)(2,1)}, bf16[1024,128]{1,0:T(8,128)(2,1)}, u32[]{:S(2)}, u32[]{:S(2)}) collective-permute-start(bf16[1024,128]{1,0:T(8,128)(2,1)} %collective-permute-done.4.refs_3_), channel_id=1, source_target_pairs={{0,64},{16,80},{32,96},{48,112},{64,128},{80,144},{96,160},{112,17... | collective-permute-start | bytes 786440 | tf_op jit(solution)/shard_map/ppermute | solution.py:536
  27.9 73.4 %collective-permute-start.10 = (bf16[1024,128]{1,0:T(8,128)(2,1)}, bf16[1024,128]{1,0:T(8,128)(2,1)S(1)}, u32[]{:S(2)}, u32[]{:S(2)}) collective-permute-start(bf16[1024,128]{1,0:T(8,128)(2,1)} %get-tuple-element.58), channel_id=1, source_target_pairs={{0,6},{2,8},{4,10},{6,12},{8,14},{10,0},{12,2},{14,4},{1,7},{3,9},... | collective-permute-start | bytes 786440 | tf_op jit(solution)/shard_map/ppermute | solution.py:540
  27.9 73.4 %copy-start.2 = (bf16[1024,128]{1,0:T(8,128)(2,1)S(1)}, bf16[1024,128]{1,0:T(8,128)(2,1)}, u32[]{:S(2)}) copy-start(bf16[1024,128]{1,0:T(8,128)(2,1)} %copy-done.1) | copy-start | bytes 786436
  27.9 73.4 %copy-start.4 = (bf16[1024,128]{1,0:T(8,128)(2,1)S(1)}, bf16[1024,128]{1,0:T(8,128)(2,1)}, u32[]{:S(2)}) copy-start(bf16[1024,128]{1,0:T(8,128)(2,1)} %copy-done.3) | copy-start | bytes 786436
  27.9 73.4 %copy-start.6 = (bf16[1024,128]{1,0:T(8,128)(2,1)S(1)}, bf16[1024,128]{1,0:T(8,128)(2,1)}, u32[]{:S(2)}) copy-start(bf16[1024,128]{1,0:T(8,128)(2,1)} %copy-done.5) | copy-start | bytes 786436
  28.0 73.4 %copy-start.8 = (s32[6]{0:T(128)S(1)}, s32[6]{0:T(128)}, u32[]{:S(2)}) copy-start(s32[6]{0:T(128)} %stack.27.meta) | copy-start | bytes 76
  28.0 73.4 %copy-start.10 = (s32[8,32]{1,0:T(8,128)S(1)}, s32[8,32]{1,0:T(8,128)}, u32[]{:S(2)}) copy-start(s32[8,32]{1,0:T(8,128)} %table.3) | copy-start | bytes 3076
  28.0 73.4 %copy-start.11 = (bf16[4,16,4096]{2,1,0:T(8,128)(2,1)S(1)}, bf16[4,16,4096]{2,1,0:T(8,128)(2,1)}, u32[]{:S(2)}) copy-start(bf16[4,16,4096]{2,1,0:T(8,128)(2,1)} %q_ref.1) | copy-start | bytes 1572868
  28.0 73.4 %copy-start.12 = (bf16[4,16,256]{2,1,0:T(8,128)(2,1)S(1)}, bf16[4,16,256]{2,1,0:T(8,128)(2,1)}, u32[]{:S(2)}) copy-start(bf16[4,16,256]{2,1,0:T(8,128)(2,1)} %nk_ref.1) | copy-start | bytes 98308
  28.0 73.4 %copy-start.13 = (bf16[4,16,256]{2,1,0:T(8,128)(2,1)S(1)}, bf16[4,16,256]{2,1,0:T(8,128)(2,1)}, u32[]{:S(2)}) copy-start(bf16[4,16,256]{2,1,0:T(8,128)(2,1)} %nv_ref.1) | copy-start | bytes 98308
  28.0 73.3 %collective-permute-start.11 = (bf16[1024,128]{1,0:T(8,128)(2,1)}, bf16[1024,128]{1,0:T(8,128)(2,1)S(1)}, u32[]{:S(2)}, u32[]{:S(2)}) collective-permute-start(bf16[1024,128]{1,0:T(8,128)(2,1)} %get-tuple-element.59), channel_id=1, source_target_pairs={{0,10},{2,12},{4,14},{6,0},{8,2},{10,4},{12,6},{14,8},{1,11},{3,13... | collective-permute-start | bytes 786440 | tf_op jit(solution)/shard_map/ppermute | solution.py:540
  104.2 0.6 copy-start.7
  104.9 68.5 %collective-permute-start.12 = (bf16[64,1152]{1,0:T(8,128)(2,1)S(1)}, bf16[64,1152]{1,0:T(8,128)(2,1)S(1)}, u32[]{:S(2)}, u32[]{:S(2)}) collective-permute-start(bf16[64,1152]{1,0:T(8,128)(2,1)S(1)} %get-tuple-element.69), channel_id=1, source_target_pairs={{0,32},{16,48},{32,0},{48,16},{64,96},{80,112},{96,64},{112,80},{1... | collective-permute-start | bytes 442376 | tf_op jit(solution)/shard_map/ppermute | solution.py:536
  104.9 68.5 %collective-permute-start.13 = (bf16[1024,128]{1,0:T(8,128)(2,1)}, bf16[1024,128]{1,0:T(8,128)(2,1)S(1)}, u32[]{:S(2)}, u32[]{:S(2)}) collective-permute-start(bf16[1024,128]{1,0:T(8,128)(2,1)} %collective-permute-done.8.refs_3_), channel_id=1, source_target_pairs={{0,192},{16,208},{32,224},{48,240},{64,0},{80,16},{96,32},{112,48}... | collective-permute-start | bytes 786440 | tf_op jit(solution)/shard_map/ppermute | solution.py:536
  173.4 0.7 copy-start.17
  173.4 5.9 %copy-start.25 = (bf16[1024,128]{1,0:T(8,128)(2,1)}, bf16[1024,128]{1,0:T(8,128)(2,1)S(1)}, u32[]{:S(2)}) copy-start(bf16[1024,128]{1,0:T(8,128)(2,1)S(1)} %collective-permute-done.13.refs_5_) | copy-start | bytes 786436
  176.0 170.7 %copy-start.9 = (s32[6]{0:T(128)S(1)}, s32[6]{0:T(128)}, u32[]{:S(2)}) copy-start(s32[6]{0:T(128)} %stack.27.meta) | copy-start | bytes 76
  176.0 160.3 %collective-permute-start.16 = (bf16[64,1152]{1,0:T(8,128)(2,1)}, bf16[64,1152]{1,0:T(8,128)(2,1)S(1)}, u32[]{:S(2)}, u32[]{:S(2)}) collective-permute-start(bf16[64,1152]{1,0:T(8,128)(2,1)} %merge.2.refs_0_), channel_id=1, source_target_pairs={{0,192},{16,208},{32,224},{48,240},{64,128},{80,144},{96,160},{112... | collective-permute-start | bytes 442376 | tf_op jit(solution)/shard_map/ppermute | solution.py:536
  176.0 160.3 %collective-permute-start.15 = (bf16[64,1152]{1,0:T(8,128)(2,1)}, bf16[64,1152]{1,0:T(8,128)(2,1)S(1)}, u32[]{:S(2)}, u32[]{:S(2)}) collective-permute-start(bf16[64,1152]{1,0:T(8,128)(2,1)} %merge.2.refs_0_), channel_id=1, source_target_pairs={{0,128},{16,144},{32,160},{48,176},{64,192},{80,208},{96,224},{112... | collective-permute-start | bytes 442376 | tf_op jit(solution)/shard_map/ppermute | solution.py:536
  176.0 160.3 %collective-permute-start.14 = (bf16[64,1152]{1,0:T(8,128)(2,1)}, bf16[64,1152]{1,0:T(8,128)(2,1)S(1)}, u32[]{:S(2)}, u32[]{:S(2)}) collective-permute-start(bf16[64,1152]{1,0:T(8,128)(2,1)} %merge.2.refs_0_), channel_id=1, source_target_pairs={{0,64},{16,80},{32,96},{48,112},{64,0},{80,16},{96,32},{112,48},{1... | collective-permute-start | bytes 442376 | tf_op jit(solution)/shard_map/ppermute | solution.py:536
  336.3 4.5 %copy-start.14 = (bf16[64,1152]{1,0:T(8,128)(2,1)}, bf16[64,1152]{1,0:T(8,128)(2,1)S(1)}, u32[]{:S(2)}) copy-start(bf16[64,1152]{1,0:T(8,128)(2,1)S(1)} %collective-permute-done.16.refs_3_) | copy-start | bytes 442372
  336.4 4.5 %copy-start.15 = (bf16[64,1152]{1,0:T(8,128)(2,1)}, bf16[64,1152]{1,0:T(8,128)(2,1)S(1)}, u32[]{:S(2)}) copy-start(bf16[64,1152]{1,0:T(8,128)(2,1)S(1)} %collective-permute-done.15.refs_2_) | copy-start | bytes 442372
  336.4 4.5 %copy-start.16 = (bf16[64,1152]{1,0:T(8,128)(2,1)}, bf16[64,1152]{1,0:T(8,128)(2,1)S(1)}, u32[]{:S(2)}) copy-start(bf16[64,1152]{1,0:T(8,128)(2,1)S(1)} %collective-permute-done.14.refs_1_) | copy-start | bytes 442372
  336.4 7.0 %collective-permute-start.17 = (bf16[256,2048]{1,0:T(8,128)(2,1)}, bf16[256,2048]{1,0:T(8,128)(2,1)S(1)}, u32[]{:S(2)}, u32[]{:S(2)}) collective-permute-start(bf16[256,2048]{1,0:T(8,128)(2,1)} %get-tuple-element.88), channel_id=1, source_target_pairs={{0,16},{16,0},{32,48},{48,32},{64,80},{80,64},{96,112},{112,96},{1... | collective-permute-start | bytes 3145736 | tf_op jit(solution)/shard_map/ppermute | solution.py:536
  343.4 7.5 %collective-permute-start.20 = (bf16[64,1024]{1,0:T(8,128)(2,1)}, bf16[64,1024]{1,0:T(8,128)(2,1)S(1)}, u32[]{:S(2)}, u32[]{:S(2)}) collective-permute-start(bf16[64,1024]{1,0:T(8,128)(2,1)} %merge.3), channel_id=1, source_target_pairs={{0,48},{16,32},{32,16},{48,0},{64,112},{80,96},{96,80},{112,64},{1... | collective-permute-start | bytes 393224 | tf_op jit(solution)/shard_map/ppermute | solution.py:536
  343.4 7.5 %collective-permute-start.19 = (bf16[64,1024]{1,0:T(8,128)(2,1)}, bf16[64,1024]{1,0:T(8,128)(2,1)S(1)}, u32[]{:S(2)}, u32[]{:S(2)}) collective-permute-start(bf16[64,1024]{1,0:T(8,128)(2,1)} %merge.3), channel_id=1, source_target_pairs={{0,16},{16,0},{32,48},{48,32},{64,80},{80,64},{96,112},{112,96},{1... | collective-permute-start | bytes 393224 | tf_op jit(solution)/shard_map/ppermute | solution.py:536
  343.9 9.6 %collective-permute-start.18 = (bf16[64,1024]{1,0:T(8,128)(2,1)}, bf16[64,1024]{1,0:T(8,128)(2,1)S(1)}, u32[]{:S(2)}, u32[]{:S(2)}) collective-permute-start(bf16[64,1024]{1,0:T(8,128)(2,1)} %merge.3), channel_id=1, source_target_pairs={{0,32},{16,48},{32,0},{48,16},{64,96},{80,112},{96,64},{112,80},{1... | collective-permute-start | bytes 393224 | tf_op jit(solution)/shard_map/ppermute | solution.py:536
  346.7 1.2 copy-start
  350.9 2.7 copy-start.18
  350.9 2.6 copy-start.19
  353.5 0.7 copy-start.20

commit v2 on v1

--- a/solution.py
+++ b/solution.py
@@ -44,7 +44,7 @@
     if first:
         q_own, q_oth, own, rr, ll, yy, state, flag, ks, vx, kbest, sem = refs
     else:
-        q_own, q_oth, ry, ly, xx, xy, before_a, flag_a, before_b, flag_b = refs[:10]
+        q_own, q_oth, yrl, xx, xy, before_a, flag_a, before_b, flag_b = refs[:9]
         o_own, o_oth, ks, vx, kbest, acc, sem = refs[-7:]
     step = pl.program_id(0)
     half = 256
@@ -53,9 +53,9 @@
         return lax.rem(xpos + dx + 4, 4) * 2 + lax.rem(ypos + dy, 2)
 
     if first:
-        pieces = [(chip_id(0, 0), own), (chip_id(-1, 0), rr), (chip_id(1, 0), ll), (chip_id(0, 1), yy)]
+        pieces = [(chip_id(0, 0), own, 0), (chip_id(-1, 0), rr, 0), (chip_id(1, 0), ll, 0), (chip_id(0, 1), yy, 0)]
     else:
-        pieces = [(chip_id(-1, 1), ry), (chip_id(1, 1), ly), (chip_id(2, 0), xx), (chip_id(2, 1), xy)]
+        pieces = [(chip_id(-1, 1), yrl, 0), (chip_id(1, 1), yrl, 1024), (chip_id(2, 0), xx, 0), (chip_id(2, 1), xy, 0)]
     needed = [p[0] <= chip for p in pieces]
     slots, count = [], jnp.int32(0)
     for need in needed:
@@ -63,11 +63,11 @@
         count = count + need.astype(jnp.int32)
 
     def copies(index):
-        buf = pieces[index][1]
+        _, buf, start = pieces[index]
         base = slots[index] * 512
         out = []
         for side in range(2):
-            off = side * 512
+            off = start + side * 512
             dst = pl.multiple_of(base + side * half, half)
             out.append(
                 pltpu.make_async_copy(
@@ -309,7 +309,9 @@
     )(meta, *parts)
 
 
-def pick_kernel(meta, table, own, f1, b1, up, down):
+def pick_kernel(meta, table, own, f1, b1, rr, ll, up, down, both):
+    both[:1024, :] = rr[...]
+    both[1024:, :] = ll[...]
     chip, core, z = meta[0], meta[1], meta[4]
     for out, shift in ((up, 3), (down, 5)):
         goal = lax.rem(z + shift, 8)
@@ -323,23 +325,24 @@
                 out[at, :] = jnp.where(rel == 1, b1[at, :], jnp.where(rel == 7, f1[at, :], own[at, :]))
 
 
-def pick(meta, table, own, f1, b1):
+def pick(meta, table, own, f1, b1, rr, ll):
     smem = pl.BlockSpec(memory_space=pltpu.SMEM)
     vmem = pl.BlockSpec(memory_space=pltpu.VMEM)
     return pl.pallas_call(
         pick_kernel,
-        in_specs=[smem, smem, vmem, vmem, vmem],
-        out_specs=[vmem, vmem],
-        out_shape=[jax.ShapeDtypeStruct((1024, HD), BF16)] * 2,
+        in_specs=[smem, smem] + [vmem] * 5,
+        out_specs=[vmem] * 3,
+        out_shape=[jax.ShapeDtypeStruct((n, HD), BF16) for n in (1024, 1024, 2048)],
+        compiler_params=pltpu.CompilerParams(vmem_limit_bytes=SMALL_LIMIT),
         name="pick",
-    )(meta, table, own, f1, b1)
+    )(meta, table, own, f1, b1, rr, ll)
 
 
 def decode_kernel(
     meta, table, q_ref, nk_ref, nv_ref, len_ref, own, f1, b1, fs, bs,
-    keep, send, ks, vx, sem,
+    out, ks, vx, sem,
 ):
-    chip, core, zpos, mask = meta[0], meta[1], meta[4], meta[5]
+    chip, core, zpos = meta[0], meta[1], meta[4]
     sources = {0: own, 7: f1, 1: b1, 2: bs, 3: bs, 4: fs, 5: fs, 6: fs}
 
     def page_copy(buf, off, page):
@@ -386,33 +389,28 @@
     keys = ks[...]
     vals = vx[...]
     lane = lax.broadcasted_iota(jnp.int32, (64, HD), 1)
-    for part, out in enumerate((keep, send)):
-        stats = jnp.zeros((64, HD), F32)
-        for g0 in range(0, 8, 4):
-            qs = []
-            for g in range(g0, g0 + 4):
-                head = (part * 8 + g) ^ mask
-                qs.append(q_ref[:, :, pl.ds(pl.multiple_of(head * HD, HD), HD)].reshape(64, HD))
-            s = dot_nt(jnp.concatenate(qs, axis=0), keys) * SCALE
-            s = jnp.where(jnp.concatenate([ok] * 4, axis=0), s, NEG)
-            best = jnp.max(s, axis=1, keepdims=True).astype(BF16).astype(F32)
-            p = jnp.exp(s - jnp.maximum(best, 0.5 * NEG)).astype(BF16)
-            o = dot_nn(p, vals)
-            for i in range(4):
-                g = g0 + i
-                at = slice(i * 64, (i + 1) * 64)
-                out[:, g * HD : (g + 1) * HD] = o[at, :HD].astype(BF16)
-                total = o[at, HD:]
-                high = total.astype(BF16).astype(F32)
-                stats = jnp.where(lane == g, best[at], stats)
-                stats = jnp.where(lane == 16 + g, high, stats)
-                stats = jnp.where(lane == 32 + g, total - high, stats)
-        out[:, 8 * HD :] = stats.astype(BF16)
+    stats = jnp.zeros((64, HD), F32)
+    for g0 in range(0, 16, 4):
+        qs = [q_ref[:, :, h * HD : (h + 1) * HD].reshape(64, HD) for h in range(g0, g0 + 4)]
+        s = dot_nt(jnp.concatenate(qs, axis=0), keys) * SCALE
+        s = jnp.where(jnp.concatenate([ok] * 4, axis=0), s, NEG)
+        best = jnp.max(s, axis=1, keepdims=True).astype(BF16).astype(F32)
+        p = jnp.exp(s - jnp.maximum(best, 0.5 * NEG)).astype(BF16)
+        o = dot_nn(p, vals)
+        for i in range(4):
+            h = g0 + i
+            at = slice(i * 64, (i + 1) * 64)
+            out[:, h * HD : (h + 1) * HD] = o[at, :HD].astype(BF16)
+            total = o[at, HD:]
+            high = total.astype(BF16).astype(F32)
+            stats = jnp.where(lane == h, best[at], stats)
+            stats = jnp.where(lane == 16 + h, high, stats)
+            stats = jnp.where(lane == 32 + h, total - high, stats)
+    out[:, 16 * HD :] = stats.astype(BF16)
 
 
 def decode_part(meta, table, dec_q, dec_k, dec_v, lens, bufs):
     any_spec = pl.BlockSpec(memory_space=pl.ANY)
-    shape = jax.ShapeDtypeStruct((64, 9 * HD), BF16)
     return pl.pallas_call(
         decode_kernel,
         grid_spec=pltpu.PrefetchScalarGridSpec(
@@ -425,27 +423,25 @@
                 pl.BlockSpec((64, 1), lambda i, m, t: (0, 0)),
             ]
             + [any_spec] * 5,
-            out_specs=[pl.BlockSpec((64, 9 * HD), lambda i, m, t: (0, 0))] * 2,
+            out_specs=pl.BlockSpec((64, 17 * HD), lambda i, m, t: (0, 0)),
             scratch_shapes=[
                 pltpu.VMEM((512 + 64, HD), BF16),
                 pltpu.VMEM((512 + 64, 2 * HD), BF16),
                 pltpu.SemaphoreType.DMA((4, 2)),
             ],
         ),
-        out_shape=[shape, shape],
+        out_shape=jax.ShapeDtypeStruct((64, 17 * HD), BF16),
         compiler_params=pltpu.CompilerParams(vmem_limit_bytes=SMALL_LIMIT),
         cost_estimate=pl.CostEstimate(flops=2 * 10**9, bytes_accessed=2**20, transcendentals=0),
         name="decode_part",
     )(meta, table, dec_q, dec_k, dec_v, lens, *bufs)
 
 
-def merge_kernel(meta, *refs, count, heads, last):
-    ins, out = refs[:count], refs[count]
-    if last:
-        held = refs[count + 1]
-        for b in range(count):
-            held[meta[2] ^ b] = ins[b][...]
-        ins = [held.at[k] for k in range(count)]
+def merge_kernel(meta, *refs, axis, count, heads, last):
+    ins, out, held = refs[:count], refs[count], refs[count + 1]
+    for b in range(count):
+        held[meta[axis] ^ b] = ins[b][...]
+    ins = [held.at[k] for k in range(count)]
     cols = heads * HD
     lane = lax.broadcasted_iota(jnp.int32, (64, HD), 1)
     stats_in = [ref[:, cols:].astype(F32) for ref in ins]
@@ -483,48 +479,41 @@
     out[:, cols:] = stats.astype(BF16)
 
 
-def merge(meta, parts, heads, last=False):
+def merge(meta, parts, axis, heads=16, last=False):
     width = heads * HD if last else (heads + 1) * HD
     vmem = pl.BlockSpec(memory_space=pltpu.VMEM)
     return pl.pallas_call(
-        functools.partial(merge_kernel, count=len(parts), heads=heads, last=last),
+        functools.partial(merge_kernel, axis=axis, count=len(parts), heads=heads, last=last),
         in_specs=[pl.BlockSpec(memory_space=pltpu.SMEM)] + [vmem] * len(parts),
         out_specs=vmem,
-        scratch_shapes=[pltpu.VMEM((len(parts), 64, (heads + 1) * HD), BF16)] if last else [],
+        scratch_shapes=[pltpu.VMEM((len(parts), 64, (heads + 1) * HD), BF16)],
         out_shape=jax.ShapeDtypeStruct((64, width), BF16),
+        compiler_params=pltpu.CompilerParams(vmem_limit_bytes=SMALL_LIMIT),
         cost_estimate=pl.CostEstimate(flops=10**6, bytes_accessed=2**18, transcendentals=0),
         name="merge",
     )(meta, *parts)
 
 
-def place_kernel(meta, *refs):
-    parts, out, sem = refs[:4], refs[4], refs[5]
-    core, mask = meta[1], meta[5]
+def place_kernel(meta, own, oth, out, sem):
     copies = []
-    for index, ref in enumerate(parts):
-        which = core if index < 2 else 1 - core
-        for b in range(4):
-            at = pl.multiple_of((which * 16 + ((index % 2 * 8 + 2 * b) ^ mask)) * HD, 2 * HD)
-            copies.append(
-                pltpu.make_async_copy(
-                    ref.at[:, :, b * 2 * HD : (b + 1) * 2 * HD], out.at[:, :, pl.ds(at, 2 * HD)], sem.at[index, b]
-                )
-            )
+    for side, ref in enumerate((own, oth)):
+        at = pl.multiple_of((meta[1] if side == 0 else 1 - meta[1]) * 16 * HD, 16 * HD)
+        copies.append(pltpu.make_async_copy(ref, out.at[:, :, pl.ds(at, 16 * HD)], sem.at[side]))
     for copy in copies:
         copy.start()
     for copy in copies:
         copy.wait()
 
 
-def place(meta, parts):
+def place(meta, own, oth):
     return pl.pallas_call(
         place_kernel,
-        in_specs=[pl.BlockSpec(memory_space=pltpu.SMEM)] + [pl.BlockSpec(memory_space=pltpu.VMEM)] * 4,
+        in_specs=[pl.BlockSpec(memory_space=pltpu.SMEM)] + [pl.BlockSpec(memory_space=pltpu.VMEM)] * 2,
         out_specs=pl.BlockSpec(memory_space=pl.ANY),
-        scratch_shapes=[pltpu.SemaphoreType.DMA((4, 4))],
+        scratch_shapes=[pltpu.SemaphoreType.DMA((2,))],
         out_shape=jax.ShapeDtypeStruct((4, 16, 4096), BF16),
         name="place",
-    )(meta, *[part.reshape(4, 16, 1024) for part in parts])
+    )(meta, own.reshape(4, 16, 2048), oth.reshape(4, 16, 2048))
 
 
 def ctx_move(array, dx=0, flip_y=0, flip_core=0, mirror_x=0):
@@ -545,8 +534,7 @@
     z = lax.axis_index("dec")
     x, y, core = c // 4, (c // 2) % 2, c % 2
     chip = c // 2
-    mask = y * 8
-    meta = jnp.stack([chip, core, x, y, z, mask]).astype(jnp.int32)
+    meta = jnp.stack([chip, core, x, y, z]).astype(jnp.int32)
 
     k0, v0 = keys[0], values[0]
     first = jnp.concatenate([k0[:, :HD], v0[:, :HD]], axis=0)
@@ -564,31 +552,29 @@
     rr, ll, yy = ctx_move(chunk, dx=1), ctx_move(chunk, dx=-1), ctx_move(chunk, flip_y=1)
     f1, b1, rr, ll, yy, lens = barrier((f1, b1, rr, ll, yy, lens))
     near = (chunk, rr, ll, yy)
-    up, down = pick(meta, page_table, chunk, f1, b1)
+    up, down, rl = pick(meta, page_table, chunk, f1, b1, rr, ll)
     fs, bs = dec_move(up, 3), dec_move(down, -3)
-    ry, ly, xx = ctx_move(yy, dx=1), ctx_move(yy, dx=-1), ctx_move(rr, dx=1)
+    yrl, xx = ctx_move(rl, flip_y=1), ctx_move(rr, dx=1)
     pa0 = prefill(meta, q, q_oth, near, 0, 8)
-    ry, ly, xx, fs, bs, pa0 = barrier((ry, ly, xx, fs, bs, pa0))
-    keep, send = decode_part(
-        meta, page_table, dec_queries, dec_keys, dec_values, lens, (chunk, f1, b1, fs, bs)
-    )
-    send, meta = barrier((send, meta))
-    got = ctx_move(send, flip_y=1)
-    xy = ctx_move(ly, dx=-1)
+    yrl, xx, fs, bs, pa0 = barrier((yrl, xx, fs, bs, pa0))
+    part = decode_part(meta, page_table, dec_queries, dec_keys, dec_values, lens, (chunk, f1, b1, fs, bs))
+    part, meta = barrier((part, meta))
+    got = [ctx_move(part, mirror_x=k) for k in (1, 2, 3)]
+    xy = ctx_move(xx, flip_y=1)
     pa1 = prefill(meta, q, q_oth, near, 8, 8)
     got, xy, pa1 = barrier((got, xy, pa1))
-    part = merge(meta, (keep, got), 8)
+    part = merge(meta, (part, *got), 2)
     part, meta = barrier((part, meta))
-    got = [ctx_move(part, mirror_x=k) for k in (1, 2, 3)]
-    own_out, oth_out = prefill(meta, q, q_oth, (ry, ly, xx, xy), 0, 16, (pa0, pa1))
+    got = ctx_move(part, flip_y=1)
+    own_out, oth_out = prefill(meta, q, q_oth, (yrl, xx, xy), 0, 16, (pa0, pa1))
     got, own_out, oth_out = barrier((got, own_out, oth_out))
     back = ctx_move(oth_out, flip_core=1)
-    part = merge(meta, (part, *got), 8, last=True)
+    part = merge(meta, (part, got), 3, last=True)
     part, back = barrier((part, back))
-    got = [ctx_move(part, flip_y=1), ctx_move(part, flip_core=1), ctx_move(part, flip_y=1, flip_core=1)]
+    got = ctx_move(part, flip_core=1)
     prefill_out = join(meta, [own_out], [back])
     got, prefill_out = barrier((got, prefill_out))
-    decode_out = place(meta, [part, *got])
+    decode_out = place(meta, part, got)
     return (prefill_out[None], decode_out)
 
 

time: 357 us -> 351 us (0.983); the launches traced: 356 us -> 347 us
  Pallas kernels: 307 us -> 303 us
  starting transfers between devices: 28.7 us -> 25 us
    ppermute x17 -> x14, starting transfers between devices: 18.4 us -> 14.9 us  [ctx_move(): return lax.ppermute(array, 'ctx', pairs)]
  transfers between devices with their start and end apart: 21 -> 18, of which waited for: 7 -> 5; matrix products, arithmetic and copies ran while one was open for 0% -> 0% of each run, Pallas kernels for 84% -> 86%
where the time goes in v2:
time: 351 us; the launch traced here: 347 us
  Pallas kernels  303 us (86%)
  starting transfers between devices  25 us (7%)
  waiting for transfers between devices  11.1 us (3%)
  local copies, waits for them, and re-layouts  6.1 us (2%)
    pallas_call x3, Pallas kernels, prefill(): pl.pallas_call(functools.partial(prefill_kernel, group=group, rows=rows,...  294 us
    ppermute x14, starting transfers between devices, ctx_move(): return lax.ppermute(array, 'ctx', pairs)  14.9 us
    ppermute x4, starting transfers between devices, dec_move(): return lax.ppermute(array, 'dec', [(i, (i + dz) % 8) for i in range(8)])  10.1 us
    ppermute x4, waiting for transfers between devices, dec_move(): return lax.ppermute(array, 'dec', [(i, (i + dz) % 8) for i in range(8)])  7.36 us
  transfers between devices with their start and end apart: 18, of which 5 were waited for; matrix products, arithmetic and copies ran while one was open for 0% of the time, Pallas kernels for 86%

profile of v2, /device:TPU:31, one launch (start us, length us, event | category | flops | bytes accessed | tf_op | source)
XLA Modules:
  0.0 346.7 jit_solution(8540371190698074091)
XLA Ops:
  0.7 1.0 fusion
  1.6 0.1 broadcast_select_fusion
  1.7 1.3 constant_dynamic-slice_fusion
  3.0 0.8 collective-permute-start.1
  3.8 0.1 collective-permute-start
  3.9 0.1 stack.23.meta
  4.0 2.3 collective-permute-done
  6.2 0.0 collective-permute-done.1.refs_1_
  6.3 0.0 copy-start.1
  6.3 1.0 collective-permute-start.6
  7.3 0.5 collective-permute-start.5
  7.9 2.1 collective-permute-start.4
  10.0 5.6 %collective-permute-start.3 = (bf16[1024,128]{1,0:T(8,128)(2,1)S(1)}, bf16[1024,128]{1,0:T(8,128)(2,1)S(1)}, u32[]{:S(2)}, u32[]{:S(2)}) collective-permute-start(bf16[1024,128]{1,0:T(8,128)(2,1)S(1)} %pad_maximum_fusion.own.refs_2_), channel_id=1, source_target_pairs={{0,14},{2,0},{4,2},{6,4},{8,6},{10,8},{12,10},{14,12},{1,15},{3,1}... | collective-permute-start | bytes 786440 | tf_op jit(solution)/shard_map/ppermute | solution.py:529
  15.6 0.0 collective-permute-start.2
  15.6 0.0 copy-done.15
  15.6 0.1 broadcast_in_dim_tile.3
  15.7 0.0 collective-permute-done.6.refs_5_
  15.7 0.1 collective-permute-done.5.ll.refs_4_
  15.7 0.0 collective-permute-done.4.rr.refs_3_
  15.7 4.2 %collective-permute-done.3.b1 = bf16[1024,128]{1,0:T(8,128)(2,1)S(1)} collective-permute-done((bf16[1024,128]{1,0:T(8,128)(2,1)S(1)}, bf16[1024,128]{1,0:T(8,128)(2,1)S(1)}, u32[]{:S(2)}, u32[]{:S(2)}) %collective-permute-start.3) | collective-permute-done | bytes 262176 | tf_op jit(solution)/shard_map/ppermute | solution.py:529
  20.0 3.1 collective-permute-done.2.f1
  23.1 0.0 copy-done.16
  23.1 0.3 collective-permute-start.8
  23.4 0.8 pick.1
  24.2 0.1 collective-permute-start.9
  24.3 4.5 %collective-permute-start.10 = (bf16[1024,128]{1,0:T(8,128)(2,1)S(1)}, bf16[1024,128]{1,0:T(8,128)(2,1)S(1)}, u32[]{:S(2)}, u32[]{:S(2)}) collective-permute-start(bf16[1024,128]{1,0:T(8,128)(2,1)S(1)} %get-tuple-element.56), channel_id=1, source_target_pairs={{0,10},{2,12},{4,14},{6,0},{8,2},{10,4},{12,6},{14,8},{1,11},{3,13... | collective-permute-start | bytes 786440 | tf_op jit(solution)/shard_map/ppermute | solution.py:529
  28.8 2.0 collective-permute-start.7
  30.8 0.0 copy-done.6
  30.8 68.3 %prefill_a.2 = (f32[8,512,256]{2,1,0:T(8,128)}, s32[4]{0:T(128)}) custom-call(s32[5]{0:T(128)} %copy-done.6, bf16[256,4096]{1,0:T(8,128)(2,1)} %bitcast.14, bf16[256,2048]{1,0:T(8,128)(2,1)} %copy-done.16, bf16[1024,128]{1,0:T(8,128)(2,1)} %copy-done.1, bf16[1024,128]{1,0:T(8,128)(2,1)} %copy-done.5, bf16[1024,128]{1,0:T(8,128)(2,1)} %copy-done.4, ...), custom_call_target="tpu_custom_call" | custom-call | flops 8589934592 | bytes 4194304 | tf_op jit(solution)/shard_map/prefill_a/pallas_call | solution.py:260
  99.1 0.1 copy.10.len_ref
  99.2 0.0 collective-permute-done.8.refs_3_
  99.2 0.0 collective-permute-done.9.fs
  99.2 0.0 collective-permute-done.10.bs
  99.3 0.0 collective-permute-done.7.refs_2_
  99.3 0.0 copy-start.2
  99.3 0.9 copy-done.2
  100.3 0.7 copy-done.7
  100.9 2.8 decode_part.1.refs_0_
  103.8 0.0 copy-start.8
  103.8 0.1 collective-permute-start.13
  103.9 0.1 collective-permute-start.12
  104.0 3.1 collective-permute-start.11
  107.1 0.0 collective-permute-start.14
  107.1 68.4 %prefill_a.3 = (f32[8,512,256]{2,1,0:T(8,128)}, s32[4]{0:T(128)}) custom-call(s32[5]{0:T(128)} %copy-done.6, bf16[256,4096]{1,0:T(8,128)(2,1)} %bitcast.15, bf16[256,2048]{1,0:T(8,128)(2,1)} %copy-done.16, bf16[1024,128]{1,0:T(8,128)(2,1)} %copy-done.1, bf16[1024,128]{1,0:T(8,128)(2,1)} %copy-done.5, bf16[1024,128]{1,0:T(8,128)(2,1)} %copy-done.4, ...), custom_call_target="tpu_custom_call" | custom-call | flops 8589934592 | bytes 4194304 | tf_op jit(solution)/shard_map/prefill_a/pallas_call | solution.py:260
  175.5 0.0 collective-permute-done.14.refs_4_
  175.6 0.0 copy-start.18
  175.6 0.0 collective-permute-done.13.refs_3_
  175.6 0.0 collective-permute-done.12.refs_2_
  175.6 0.0 collective-permute-done.11.refs_1_
  175.6 1.3 merge.2.refs_0_
  176.9 0.1 collective-permute-start.15
  177.1 0.0 copy-done.18
  177.1 156.8 %prefill_b.1 = (bf16[256,2048]{1,0:T(8,128)(2,1)}, bf16[256,2048]{1,0:T(8,128)(2,1)}) custom-call(s32[5]{0:T(128)} %copy-done.6, bf16[256,4096]{1,0:T(8,128)(2,1)} %bitcast.16, bf16[256,2048]{1,0:T(8,128)(2,1)} %copy-done.16, bf16[2048,128]{1,0:T(8,128)(2,1)} %collective-permute-done.7.refs_2_, bf16[1024,128]{1,0:T(8,128)(2,1)} %collective-permute-done.8.refs_3_, ...), custom_call_target="tpu_custom_call" | custom-call | flops 17179869184 | bytes 4194304 | tf_op jit(solution)/shard_map/prefill_b/pallas_call | solution.py:260
  333.8 0.0 collective-permute-done.15.refs_1_
  333.8 4.2 %collective-permute-start.16 = (bf16[256,2048]{1,0:T(8,128)(2,1)}, bf16[256,2048]{1,0:T(8,128)(2,1)S(1)}, u32[]{:S(2)}, u32[]{:S(2)}) collective-permute-start(bf16[256,2048]{1,0:T(8,128)(2,1)} %get-tuple-element.82), channel_id=1, source_target_pairs={{0,16},{16,0},{32,48},{48,32},{64,80},{80,64},{96,112},{112,96},{1... | collective-permute-start | bytes 3145736 | tf_op jit(solution)/shard_map/ppermute | solution.py:525
  338.0 0.0 copy-done.9
  338.0 1.1 merge.3
  339.1 1.4 collective-permute-done.16.refs_1_
  340.5 0.4 collective-permute-start.17
  340.9 1.2 copy-done
  342.1 1.9 join.1
  344.0 0.0 collective-permute-done.17
  344.0 0.7 copy-done.14
  344.7 1.8 place.1
  (27 shorter events, 0.1 us)
Async XLA Ops:
  0.6 14.9 %copy-start.15 = (s32[16]{0:T(128)S(1)}, s32[16]{0:T(128)}, u32[]{:S(2)}) copy-start(s32[16]{0:T(128)} %param.15) | copy-start | bytes 196
  0.6 22.7 %copy-start.10 = (s32[8,32]{1,0:T(8,128)S(1)}, s32[8,32]{1,0:T(8,128)}, u32[]{:S(2)}) copy-start(s32[8,32]{1,0:T(8,128)} %table.3) | copy-start | bytes 3076
  3.0 3.2 collective-permute-start.1
  3.8 2.5 collective-permute-start
  3.9 26.8 %copy-start.6 = (s32[5]{0:T(128)}, s32[5]{0:T(128)S(1)}, u32[]{:S(2)}) copy-start(s32[5]{0:T(128)S(1)} %stack.23.meta) | copy-start | bytes 64
  6.2 16.8 %copy-start.16 = (bf16[256,2048]{1,0:T(8,128)(2,1)}, bf16[256,2048]{1,0:T(8,128)(2,1)S(1)}, u32[]{:S(2)}) copy-start(bf16[256,2048]{1,0:T(8,128)(2,1)S(1)} %collective-permute-done.1.refs_1_) | copy-start | bytes 3145732
  6.3 24.5 %copy-start.1 = (bf16[1024,128]{1,0:T(8,128)(2,1)}, bf16[1024,128]{1,0:T(8,128)(2,1)S(1)}, u32[]{:S(2)}) copy-start(bf16[1024,128]{1,0:T(8,128)(2,1)S(1)} %pad_maximum_fusion.own.refs_2_) | copy-start | bytes 786436
  6.3 9.4 %collective-permute-start.6 = (bf16[1024,128]{1,0:T(8,128)(2,1)S(1)}, bf16[1024,128]{1,0:T(8,128)(2,1)S(1)}, u32[]{:S(2)}, u32[]{:S(2)}) collective-permute-start(bf16[1024,128]{1,0:T(8,128)(2,1)S(1)} %pad_maximum_fusion.own.refs_2_), channel_id=1, source_target_pairs={{0,32},{16,48},{32,0},{48,16},{64,96},{80,112},{96,64},{112,80},{1... | collective-permute-start | bytes 786440 | tf_op jit(solution)/shard_map/ppermute | solution.py:525
  7.3 8.4 %collective-permute-start.5 = (bf16[1024,128]{1,0:T(8,128)(2,1)S(1)}, bf16[1024,128]{1,0:T(8,128)(2,1)S(1)}, u32[]{:S(2)}, u32[]{:S(2)}) collective-permute-start(bf16[1024,128]{1,0:T(8,128)(2,1)S(1)} %pad_maximum_fusion.own.refs_2_), channel_id=1, source_target_pairs={{0,192},{16,208},{32,224},{48,240},{64,0},{80,16},{96,32},{112,48}... | collective-permute-start | bytes 786440 | tf_op jit(solution)/shard_map/ppermute | solution.py:525
  7.9 7.9 %collective-permute-start.4 = (bf16[1024,128]{1,0:T(8,128)(2,1)S(1)}, bf16[1024,128]{1,0:T(8,128)(2,1)S(1)}, u32[]{:S(2)}, u32[]{:S(2)}) collective-permute-start(bf16[1024,128]{1,0:T(8,128)(2,1)S(1)} %pad_maximum_fusion.own.refs_2_), channel_id=1, source_target_pairs={{0,64},{16,80},{32,96},{48,112},{64,128},{80,144},{96,160},{112,17... | collective-permute-start | bytes 786440 | tf_op jit(solution)/shard_map/ppermute | solution.py:525
  10.0 10.0 %collective-permute-start.3 = (bf16[1024,128]{1,0:T(8,128)(2,1)S(1)}, bf16[1024,128]{1,0:T(8,128)(2,1)S(1)}, u32[]{:S(2)}, u32[]{:S(2)}) collective-permute-start(bf16[1024,128]{1,0:T(8,128)(2,1)S(1)} %pad_maximum_fusion.own.refs_2_), channel_id=1, source_target_pairs={{0,14},{2,0},{4,2},{6,4},{8,6},{10,8},{12,10},{14,12},{1,15},{3,1}... | collective-permute-start | bytes 786440 | tf_op jit(solution)/shard_map/ppermute | solution.py:529
  15.6 7.5 %collective-permute-start.2 = (bf16[1024,128]{1,0:T(8,128)(2,1)S(1)}, bf16[1024,128]{1,0:T(8,128)(2,1)S(1)}, u32[]{:S(2)}, u32[]{:S(2)}) collective-permute-start(bf16[1024,128]{1,0:T(8,128)(2,1)S(1)} %pad_maximum_fusion.own.refs_2_), channel_id=1, source_target_pairs={{0,2},{2,4},{4,6},{6,8},{8,10},{10,12},{12,14},{14,0},{1,3},{3,5},... | collective-permute-start | bytes 786440 | tf_op jit(solution)/shard_map/ppermute | solution.py:529
  15.7 8.5 %copy-start.17 = (bf16[1024,128]{1,0:T(8,128)(2,1)}, bf16[1024,128]{1,0:T(8,128)(2,1)S(1)}, u32[]{:S(2)}) copy-start(bf16[1024,128]{1,0:T(8,128)(2,1)S(1)} %collective-permute-done.6.refs_5_) | copy-start | bytes 786436
  15.7 15.1 %copy-start.4 = (bf16[1024,128]{1,0:T(8,128)(2,1)}, bf16[1024,128]{1,0:T(8,128)(2,1)S(1)}, u32[]{:S(2)}) copy-start(bf16[1024,128]{1,0:T(8,128)(2,1)S(1)} %collective-permute-done.5.ll.refs_4_) | copy-start | bytes 786436
  15.7 15.1 %copy-start.5 = (bf16[1024,128]{1,0:T(8,128)(2,1)}, bf16[1024,128]{1,0:T(8,128)(2,1)S(1)}, u32[]{:S(2)}) copy-start(bf16[1024,128]{1,0:T(8,128)(2,1)S(1)} %collective-permute-done.4.rr.refs_3_) | copy-start | bytes 786436
  23.1 76.2 %collective-permute-start.8 = (bf16[1024,128]{1,0:T(8,128)(2,1)S(1)}, bf16[1024,128]{1,0:T(8,128)(2,1)}, u32[]{:S(2)}, u32[]{:S(2)}) collective-permute-start(bf16[1024,128]{1,0:T(8,128)(2,1)S(1)} %collective-permute-done.4.rr.refs_3_), channel_id=1, source_target_pairs={{0,64},{16,80},{32,96},{48,112},{64,128},{80,144},{96,160},{112,17... | collective-permute-start | bytes 786440 | tf_op jit(solution)/shard_map/ppermute | solution.py:525
  24.2 75.0 %collective-permute-start.9 = (bf16[1024,128]{1,0:T(8,128)(2,1)S(1)}, bf16[1024,128]{1,0:T(8,128)(2,1)S(1)}, u32[]{:S(2)}, u32[]{:S(2)}) collective-permute-start(bf16[1024,128]{1,0:T(8,128)(2,1)S(1)} %get-tuple-element.55), channel_id=1, source_target_pairs={{0,6},{2,8},{4,10},{6,12},{8,14},{10,0},{12,2},{14,4},{1,7},{3,9},... | collective-permute-start | bytes 786440 | tf_op jit(solution)/shard_map/ppermute | solution.py:529
  24.3 74.9 %collective-permute-start.10 = (bf16[1024,128]{1,0:T(8,128)(2,1)S(1)}, bf16[1024,128]{1,0:T(8,128)(2,1)S(1)}, u32[]{:S(2)}, u32[]{:S(2)}) collective-permute-start(bf16[1024,128]{1,0:T(8,128)(2,1)S(1)} %get-tuple-element.56), channel_id=1, source_target_pairs={{0,10},{2,12},{4,14},{6,0},{8,2},{10,4},{12,6},{14,8},{1,11},{3,13... | collective-permute-start | bytes 786440 | tf_op jit(solution)/shard_map/ppermute | solution.py:529
  28.8 70.5 %copy-start.11 = (bf16[4,16,4096]{2,1,0:T(8,128)(2,1)S(1)}, bf16[4,16,4096]{2,1,0:T(8,128)(2,1)}, u32[]{:S(2)}) copy-start(bf16[4,16,4096]{2,1,0:T(8,128)(2,1)} %q_ref.1) | copy-start | bytes 1572868
  28.8 70.5 %copy-start.12 = (bf16[4,16,256]{2,1,0:T(8,128)(2,1)S(1)}, bf16[4,16,256]{2,1,0:T(8,128)(2,1)}, u32[]{:S(2)}) copy-start(bf16[4,16,256]{2,1,0:T(8,128)(2,1)} %nk_ref.1) | copy-start | bytes 98308
  28.8 70.5 %copy-start.13 = (bf16[4,16,256]{2,1,0:T(8,128)(2,1)S(1)}, bf16[4,16,256]{2,1,0:T(8,128)(2,1)}, u32[]{:S(2)}) copy-start(bf16[4,16,256]{2,1,0:T(8,128)(2,1)} %nv_ref.1) | copy-start | bytes 98308
  28.8 70.5 %collective-permute-start.7 = (bf16[2048,128]{1,0:T(8,128)(2,1)S(1)}, bf16[2048,128]{1,0:T(8,128)(2,1)}, u32[]{:S(2)}, u32[]{:S(2)}) collective-permute-start(bf16[2048,128]{1,0:T(8,128)(2,1)S(1)} %get-tuple-element.54), channel_id=1, source_target_pairs={{0,32},{16,48},{32,0},{48,16},{64,96},{80,112},{96,64},{112,80},{1... | collective-permute-start | bytes 1572872 | tf_op jit(solution)/shard_map/ppermute | solution.py:525
  99.3 1.0 copy-start.2
  100.3 0.7 copy-start.7
  103.8 71.8 %copy-start.8 = (s32[5]{0:T(128)S(1)}, s32[5]{0:T(128)}, u32[]{:S(2)}) copy-start(s32[5]{0:T(128)} %copy-done.6) | copy-start | bytes 64
  103.8 71.8 %collective-permute-start.13 = (bf16[64,2176]{1,0:T(8,128)(2,1)S(1)}, bf16[64,2176]{1,0:T(8,128)(2,1)S(1)}, u32[]{:S(2)}, u32[]{:S(2)}) collective-permute-start(bf16[64,2176]{1,0:T(8,128)(2,1)S(1)} %decode_part.1.refs_0_), channel_id=1, source_target_pairs={{0,192},{16,208},{32,224},{48,240},{64,128},{80,144},{96,160},{112... | collective-permute-start | bytes 835592 | tf_op jit(solution)/shard_map/ppermute | solution.py:525
  103.9 71.7 %collective-permute-start.12 = (bf16[64,2176]{1,0:T(8,128)(2,1)S(1)}, bf16[64,2176]{1,0:T(8,128)(2,1)S(1)}, u32[]{:S(2)}, u32[]{:S(2)}) collective-permute-start(bf16[64,2176]{1,0:T(8,128)(2,1)S(1)} %decode_part.1.refs_0_), channel_id=1, source_target_pairs={{0,128},{16,144},{32,160},{48,176},{64,192},{80,208},{96,224},{112... | collective-permute-start | bytes 835592 | tf_op jit(solution)/shard_map/ppermute | solution.py:525
  104.0 71.6 %collective-permute-start.11 = (bf16[64,2176]{1,0:T(8,128)(2,1)S(1)}, bf16[64,2176]{1,0:T(8,128)(2,1)S(1)}, u32[]{:S(2)}, u32[]{:S(2)}) collective-permute-start(bf16[64,2176]{1,0:T(8,128)(2,1)S(1)} %decode_part.1.refs_0_), channel_id=1, source_target_pairs={{0,64},{16,80},{32,96},{48,112},{64,0},{80,16},{96,32},{112,48},{1... | collective-permute-start | bytes 835592 | tf_op jit(solution)/shard_map/ppermute | solution.py:525
  107.1 68.4 %collective-permute-start.14 = (bf16[1024,128]{1,0:T(8,128)(2,1)}, bf16[1024,128]{1,0:T(8,128)(2,1)S(1)}, u32[]{:S(2)}, u32[]{:S(2)}) collective-permute-start(bf16[1024,128]{1,0:T(8,128)(2,1)} %collective-permute-done.8.refs_3_), channel_id=1, source_target_pairs={{0,32},{16,48},{32,0},{48,16},{64,96},{80,112},{96,64},{112,80},{1... | collective-permute-start | bytes 786440 | tf_op jit(solution)/shard_map/ppermute | solution.py:525
  175.6 1.5 copy-start.18
  176.9 161.1 %copy-start.9 = (s32[5]{0:T(128)S(1)}, s32[5]{0:T(128)}, u32[]{:S(2)}) copy-start(s32[5]{0:T(128)} %copy-done.6) | copy-start | bytes 64
  176.9 156.9 %collective-permute-start.15 = (bf16[64,2176]{1,0:T(8,128)(2,1)S(1)}, bf16[64,2176]{1,0:T(8,128)(2,1)S(1)}, u32[]{:S(2)}, u32[]{:S(2)}) collective-permute-start(bf16[64,2176]{1,0:T(8,128)(2,1)S(1)} %merge.2.refs_0_), channel_id=1, source_target_pairs={{0,32},{16,48},{32,0},{48,16},{64,96},{80,112},{96,64},{112,80},{1... | collective-permute-start | bytes 835592 | tf_op jit(solution)/shard_map/ppermute | solution.py:525
  333.8 6.7 %collective-permute-start.16 = (bf16[256,2048]{1,0:T(8,128)(2,1)}, bf16[256,2048]{1,0:T(8,128)(2,1)S(1)}, u32[]{:S(2)}, u32[]{:S(2)}) collective-permute-start(bf16[256,2048]{1,0:T(8,128)(2,1)} %get-tuple-element.82), channel_id=1, source_target_pairs={{0,16},{16,0},{32,48},{48,32},{64,80},{80,64},{96,112},{112,96},{1... | collective-permute-start | bytes 3145736 | tf_op jit(solution)/shard_map/ppermute | solution.py:525
  339.1 4.9 %copy-start.3 = (bf16[64,2048]{1,0:T(8,128)(2,1)}, bf16[64,2048]{1,0:T(8,128)(2,1)S(1)}, u32[]{:S(2)}) copy-start(bf16[64,2048]{1,0:T(8,128)(2,1)S(1)} %merge.3) | copy-start | bytes 786436
  340.5 3.5 %collective-permute-start.17 = (bf16[64,2048]{1,0:T(8,128)(2,1)S(1)}, bf16[64,2048]{1,0:T(8,128)(2,1)S(1)}, u32[]{:S(2)}, u32[]{:S(2)}) collective-permute-start(bf16[64,2048]{1,0:T(8,128)(2,1)S(1)} %merge.3), channel_id=1, source_target_pairs={{0,16},{16,0},{32,48},{48,32},{64,80},{80,64},{96,112},{112,96},{1... | collective-permute-start | bytes 786440 | tf_op jit(solution)/shard_map/ppermute | solution.py:525
  340.9 1.2 copy-start
  344.0 0.7 copy-start.14

commit v3 on v2

--- a/solution.py
+++ b/solution.py
@@ -119,12 +119,22 @@
         shifted = jnp.where(later, flag_b[lax.rem(step, flag_b.shape[0])], flag_a[lax.rem(step, flag_a.shape[0])]) != 0
         safe = safe & jnp.logical_not(shifted)
 
-    def tiles():
-        for g in range(group):
+    def tiles(pair):
+        for i in range(2):
+            g = pair * 2 + i
+            cols = pl.ds(pl.multiple_of(g * HD, HD), HD)
             for side in range(2):
                 for r in range(half // rows):
-                    q = q_refs[side][r * rows : (r + 1) * rows, g * HD : (g + 1) * HD]
+                    q = q_refs[side][r * rows : (r + 1) * rows, cols]
                     yield g, side, r, slice(side * half + r * rows, side * half + (r + 1) * rows), q
+
+    def over_pairs(work):
+        def one_pair(pair, carry):
+            for tile in tiles(pair):
+                work(*tile)
+            return carry
+
+        lax.fori_loop(0, group // 2, one_pair, 0)
 
     def allowed(side, r):
         q_pos0 = (core if side == 0 else 1 - core) * half + r * rows
@@ -140,7 +150,7 @@
         return dot_nn(p.astype(BF16), vx[pl.ds(base, size), :])
 
     def write(g, side, at, both):
-        cols = slice(g * HD, (g + 1) * HD)
+        cols = pl.ds(pl.multiple_of(g * HD, HD), HD)
         r = slice(at.start - side * half, at.stop - side * half)
         (o_own, o_oth)[side][r, cols] = (both[:, :HD] / both[:, HD:]).astype(BF16)
 
@@ -152,30 +162,36 @@
 
     @pl.when(safe & full)
     def _straight():
-        for g, side, r, at, q in tiles():
+        def work(g, side, r, at, q):
             if first:
                 state[g, at, :] = weighted(q, 0, 2048, allowed(side, r))
             else:
                 write(g, side, at, started(g, at) + weighted(q, 0, 2048))
 
+        over_pairs(work)
+
     @pl.when(safe & jnp.logical_not(full))
     def _plain():
         sums = state if first else acc
-        for g, side, r, at, q in tiles():
+
+        def start(g, side, r, at, q):
             if first:
                 sums[g, at, :] = weighted(q, 0, 512, allowed(side, r))
             else:
                 sums[g, at, :] = started(g, at)
 
+        over_pairs(start)
+
         def one(index, carry):
-            for g, side, r, at, q in tiles():
+            def add(g, side, r, at, q):
                 sums[g, at, :] += weighted(q, pl.multiple_of(index * 512, 512), 512)
+
+            over_pairs(add)
             return carry
 
         lax.fori_loop(1 if first else 0, count, one, 0)
         if not first:
-            for g, side, r, at, q in tiles():
-                write(g, side, at, sums[g, at, :])
+            over_pairs(lambda g, side, r, at, q: write(g, side, at, sums[g, at, :]))
 
     @pl.when(jnp.logical_not(safe))
     def _online():
@@ -223,7 +239,7 @@
             lax.fori_loop(0, group * (half // rows), tile, 0)
 
 
-def prefill(meta, queries, q_oth, bufs, head, heads, before=None, group=2, rows=128):
+def prefill(meta, queries, q_oth, bufs, head, heads, before=None, group=4, rows=128):
     per = 16 // group
     at = head // group
     first = before is None

time: 351 us -> 350 us (level)
  no operation moved by 1% of the time
where the time goes in v3:
time: 350 us; the launch traced here: 347 us
  Pallas kernels  303 us (87%)
  starting transfers between devices  25 us (7%)
  waiting for transfers between devices  11.1 us (3%)
  local copies, waits for them, and re-layouts  6.1 us (2%)
    pallas_call x3, Pallas kernels, prefill(): pl.pallas_call(functools.partial(prefill_kernel, group=group, rows=rows,...  293 us
    ppermute x14, starting transfers between devices, ctx_move(): return lax.ppermute(array, 'ctx', pairs)  14.8 us
    ppermute x4, starting transfers between devices, dec_move(): return lax.ppermute(array, 'dec', [(i, (i + dz) % 8) for i in range(8)])  10.1 us
    ppermute x4, waiting for transfers between devices, dec_move(): return lax.ppermute(array, 'dec', [(i, (i + dz) % 8) for i in range(8)])  7.36 us
  transfers between devices with their start and end apart: 18, of which 5 were waited for; matrix products, arithmetic and copies ran while one was open for 0% of the time, Pallas kernels for 86%

profile of v3, /device:TPU:31, one launch (start us, length us, event | category | flops | bytes accessed | tf_op | source)
XLA Modules:
  0.0 346.6 jit_solution(14059628664696523195)
XLA Ops:
  0.6 0.0 copy-start.15
  0.7 1.0 fusion
  1.6 0.1 broadcast_select_fusion
  1.7 1.3 constant_dynamic-slice_fusion
  3.0 0.8 collective-permute-start.1
  3.8 0.1 collective-permute-start
  3.9 0.1 stack.23.meta
  4.0 2.3 collective-permute-done
  6.2 0.0 collective-permute-done.1.refs_1_
  6.3 0.0 copy-start.1
  6.3 1.0 collective-permute-start.6
  7.3 0.5 collective-permute-start.5
  7.9 2.1 collective-permute-start.4
  10.0 5.6 %collective-permute-start.3 = (bf16[1024,128]{1,0:T(8,128)(2,1)S(1)}, bf16[1024,128]{1,0:T(8,128)(2,1)S(1)}, u32[]{:S(2)}, u32[]{:S(2)}) collective-permute-start(bf16[1024,128]{1,0:T(8,128)(2,1)S(1)} %pad_maximum_fusion.own.refs_2_), channel_id=1, source_target_pairs={{0,14},{2,0},{4,2},{6,4},{8,6},{10,8},{12,10},{14,12},{1,15},{3,1}... | collective-permute-start | bytes 786440 | tf_op jit(solution)/shard_map/ppermute | solution.py:545
  15.6 0.0 collective-permute-start.2
  15.6 0.0 copy-done.15
  15.6 0.1 broadcast_in_dim_tile.3
  15.7 0.0 collective-permute-done.6.refs_5_
  15.7 0.1 collective-permute-done.5.ll.refs_4_
  15.7 0.0 collective-permute-done.4.rr.refs_3_
  15.7 4.2 %collective-permute-done.3.b1 = bf16[1024,128]{1,0:T(8,128)(2,1)S(1)} collective-permute-done((bf16[1024,128]{1,0:T(8,128)(2,1)S(1)}, bf16[1024,128]{1,0:T(8,128)(2,1)S(1)}, u32[]{:S(2)}, u32[]{:S(2)}) %collective-permute-start.3) | collective-permute-done | bytes 262176 | tf_op jit(solution)/shard_map/ppermute | solution.py:545
  20.0 3.1 collective-permute-done.2.f1
  23.1 0.0 copy-done.16
  23.1 0.3 collective-permute-start.8
  23.4 0.8 pick.1
  24.2 0.1 collective-permute-start.9
  24.3 4.5 %collective-permute-start.10 = (bf16[1024,128]{1,0:T(8,128)(2,1)S(1)}, bf16[1024,128]{1,0:T(8,128)(2,1)S(1)}, u32[]{:S(2)}, u32[]{:S(2)}) collective-permute-start(bf16[1024,128]{1,0:T(8,128)(2,1)S(1)} %get-tuple-element.56), channel_id=1, source_target_pairs={{0,10},{2,12},{4,14},{6,0},{8,2},{10,4},{12,6},{14,8},{1,11},{3,13... | collective-permute-start | bytes 786440 | tf_op jit(solution)/shard_map/ppermute | solution.py:545
  28.8 2.0 collective-permute-start.7
  30.8 0.0 copy-done.6
  30.8 68.3 %prefill_a.2 = (f32[8,512,256]{2,1,0:T(8,128)}, s32[2]{0:T(128)}) custom-call(s32[5]{0:T(128)} %copy-done.6, bf16[256,4096]{1,0:T(8,128)(2,1)} %bitcast.14, bf16[256,2048]{1,0:T(8,128)(2,1)} %copy-done.16, bf16[1024,128]{1,0:T(8,128)(2,1)} %copy-done.1, bf16[1024,128]{1,0:T(8,128)(2,1)} %copy-done.5, bf16[1024,128]{1,0:T(8,128)(2,1)} %copy-done.4, ...), custom_call_target="tpu_custom_call" | custom-call | flops 8589934592 | bytes 4194304 | tf_op jit(solution)/shard_map/prefill_a/pallas_call | solution.py:276
  99.1 0.1 copy.10.len_ref
  99.2 0.0 collective-permute-done.8.refs_3_
  99.2 0.0 collective-permute-done.9.fs
  99.2 0.0 collective-permute-done.10.bs
  99.2 0.0 collective-permute-done.7.refs_2_
  99.2 0.0 copy-start.2
  99.3 0.9 copy-done.2
  100.2 0.7 copy-done.7
  100.9 2.8 decode_part.1.refs_0_
  103.7 0.1 collective-permute-start.13
  103.8 0.1 collective-permute-start.12
  103.9 3.1 collective-permute-start.11
  107.0 0.0 collective-permute-start.14
  107.1 68.3 %prefill_a.3 = (f32[8,512,256]{2,1,0:T(8,128)}, s32[2]{0:T(128)}) custom-call(s32[5]{0:T(128)} %copy-done.6, bf16[256,4096]{1,0:T(8,128)(2,1)} %bitcast.15, bf16[256,2048]{1,0:T(8,128)(2,1)} %copy-done.16, bf16[1024,128]{1,0:T(8,128)(2,1)} %copy-done.1, bf16[1024,128]{1,0:T(8,128)(2,1)} %copy-done.5, bf16[1024,128]{1,0:T(8,128)(2,1)} %copy-done.4, ...), custom_call_target="tpu_custom_call" | custom-call | flops 8589934592 | bytes 4194304 | tf_op jit(solution)/shard_map/prefill_a/pallas_call | solution.py:276
  175.4 0.0 collective-permute-done.14.refs_4_
  175.4 0.0 copy-start.18
  175.4 0.0 collective-permute-done.13.refs_3_
  175.4 0.0 collective-permute-done.12.refs_2_
  175.5 0.0 collective-permute-done.11.refs_1_
  175.5 1.3 merge.2.refs_0_
  176.8 0.0 copy-start.9
  176.8 0.1 collective-permute-start.15
  176.9 156.7 %prefill_b.1 = (bf16[256,2048]{1,0:T(8,128)(2,1)}, bf16[256,2048]{1,0:T(8,128)(2,1)}) custom-call(s32[5]{0:T(128)} %copy-done.6, bf16[256,4096]{1,0:T(8,128)(2,1)} %bitcast.16, bf16[256,2048]{1,0:T(8,128)(2,1)} %copy-done.16, bf16[2048,128]{1,0:T(8,128)(2,1)} %collective-permute-done.7.refs_2_, bf16[1024,128]{1,0:T(8,128)(2,1)} %collective-permute-done.8.refs_3_, ...), custom_call_target="tpu_custom_call" | custom-call | flops 17179869184 | bytes 4194304 | tf_op jit(solution)/shard_map/prefill_b/pallas_call | solution.py:276
  333.7 0.0 collective-permute-done.15.refs_1_
  333.7 4.2 %collective-permute-start.16 = (bf16[256,2048]{1,0:T(8,128)(2,1)}, bf16[256,2048]{1,0:T(8,128)(2,1)S(1)}, u32[]{:S(2)}, u32[]{:S(2)}) collective-permute-start(bf16[256,2048]{1,0:T(8,128)(2,1)} %get-tuple-element.82), channel_id=1, source_target_pairs={{0,16},{16,0},{32,48},{48,32},{64,80},{80,64},{96,112},{112,96},{1... | collective-permute-start | bytes 3145736 | tf_op jit(solution)/shard_map/ppermute | solution.py:541
  337.9 1.1 merge.3
  339.0 1.4 collective-permute-done.16.refs_1_
  340.4 0.4 collective-permute-start.17
  340.7 1.2 copy-done
  342.0 1.9 join.1
  343.9 0.0 collective-permute-done.17
  343.9 0.0 copy-start.14
  343.9 0.7 copy-done.14
  344.6 1.8 place.1
  (27 shorter events, 0.1 us)
Async XLA Ops:
  0.6 14.9 %copy-start.15 = (s32[16]{0:T(128)S(1)}, s32[16]{0:T(128)}, u32[]{:S(2)}) copy-start(s32[16]{0:T(128)} %param.15) | copy-start | bytes 196
  0.6 22.7 %copy-start.10 = (s32[8,32]{1,0:T(8,128)S(1)}, s32[8,32]{1,0:T(8,128)}, u32[]{:S(2)}) copy-start(s32[8,32]{1,0:T(8,128)} %table.3) | copy-start | bytes 3076
  3.0 3.2 collective-permute-start.1
  3.8 2.5 collective-permute-start
  3.9 26.8 %copy-start.6 = (s32[5]{0:T(128)}, s32[5]{0:T(128)S(1)}, u32[]{:S(2)}) copy-start(s32[5]{0:T(128)S(1)} %stack.23.meta) | copy-start | bytes 64
  6.2 16.8 %copy-start.16 = (bf16[256,2048]{1,0:T(8,128)(2,1)}, bf16[256,2048]{1,0:T(8,128)(2,1)S(1)}, u32[]{:S(2)}) copy-start(bf16[256,2048]{1,0:T(8,128)(2,1)S(1)} %collective-permute-done.1.refs_1_) | copy-start | bytes 3145732
  6.3 24.5 %copy-start.1 = (bf16[1024,128]{1,0:T(8,128)(2,1)}, bf16[1024,128]{1,0:T(8,128)(2,1)S(1)}, u32[]{:S(2)}) copy-start(bf16[1024,128]{1,0:T(8,128)(2,1)S(1)} %pad_maximum_fusion.own.refs_2_) | copy-start | bytes 786436
  6.3 9.4 %collective-permute-start.6 = (bf16[1024,128]{1,0:T(8,128)(2,1)S(1)}, bf16[1024,128]{1,0:T(8,128)(2,1)S(1)}, u32[]{:S(2)}, u32[]{:S(2)}) collective-permute-start(bf16[1024,128]{1,0:T(8,128)(2,1)S(1)} %pad_maximum_fusion.own.refs_2_), channel_id=1, source_target_pairs={{0,32},{16,48},{32,0},{48,16},{64,96},{80,112},{96,64},{112,80},{1... | collective-permute-start | bytes 786440 | tf_op jit(solution)/shard_map/ppermute | solution.py:541
  7.3 8.4 %collective-permute-start.5 = (bf16[1024,128]{1,0:T(8,128)(2,1)S(1)}, bf16[1024,128]{1,0:T(8,128)(2,1)S(1)}, u32[]{:S(2)}, u32[]{:S(2)}) collective-permute-start(bf16[1024,128]{1,0:T(8,128)(2,1)S(1)} %pad_maximum_fusion.own.refs_2_), channel_id=1, source_target_pairs={{0,192},{16,208},{32,224},{48,240},{64,0},{80,16},{96,32},{112,48}... | collective-permute-start | bytes 786440 | tf_op jit(solution)/shard_map/ppermute | solution.py:541
  7.9 7.9 %collective-permute-start.4 = (bf16[1024,128]{1,0:T(8,128)(2,1)S(1)}, bf16[1024,128]{1,0:T(8,128)(2,1)S(1)}, u32[]{:S(2)}, u32[]{:S(2)}) collective-permute-start(bf16[1024,128]{1,0:T(8,128)(2,1)S(1)} %pad_maximum_fusion.own.refs_2_), channel_id=1, source_target_pairs={{0,64},{16,80},{32,96},{48,112},{64,128},{80,144},{96,160},{112,17... | collective-permute-start | bytes 786440 | tf_op jit(solution)/shard_map/ppermute | solution.py:541
  10.0 10.0 %collective-permute-start.3 = (bf16[1024,128]{1,0:T(8,128)(2,1)S(1)}, bf16[1024,128]{1,0:T(8,128)(2,1)S(1)}, u32[]{:S(2)}, u32[]{:S(2)}) collective-permute-start(bf16[1024,128]{1,0:T(8,128)(2,1)S(1)} %pad_maximum_fusion.own.refs_2_), channel_id=1, source_target_pairs={{0,14},{2,0},{4,2},{6,4},{8,6},{10,8},{12,10},{14,12},{1,15},{3,1}... | collective-permute-start | bytes 786440 | tf_op jit(solution)/shard_map/ppermute | solution.py:545
  15.6 7.5 %collective-permute-start.2 = (bf16[1024,128]{1,0:T(8,128)(2,1)S(1)}, bf16[1024,128]{1,0:T(8,128)(2,1)S(1)}, u32[]{:S(2)}, u32[]{:S(2)}) collective-permute-start(bf16[1024,128]{1,0:T(8,128)(2,1)S(1)} %pad_maximum_fusion.own.refs_2_), channel_id=1, source_target_pairs={{0,2},{2,4},{4,6},{6,8},{8,10},{10,12},{12,14},{14,0},{1,3},{3,5},... | collective-permute-start | bytes 786440 | tf_op jit(solution)/shard_map/ppermute | solution.py:545
  15.7 8.5 %copy-start.17 = (bf16[1024,128]{1,0:T(8,128)(2,1)}, bf16[1024,128]{1,0:T(8,128)(2,1)S(1)}, u32[]{:S(2)}) copy-start(bf16[1024,128]{1,0:T(8,128)(2,1)S(1)} %collective-permute-done.6.refs_5_) | copy-start | bytes 786436
  15.7 15.1 %copy-start.4 = (bf16[1024,128]{1,0:T(8,128)(2,1)}, bf16[1024,128]{1,0:T(8,128)(2,1)S(1)}, u32[]{:S(2)}) copy-start(bf16[1024,128]{1,0:T(8,128)(2,1)S(1)} %collective-permute-done.5.ll.refs_4_) | copy-start | bytes 786436
  15.7 15.1 %copy-start.5 = (bf16[1024,128]{1,0:T(8,128)(2,1)}, bf16[1024,128]{1,0:T(8,128)(2,1)S(1)}, u32[]{:S(2)}) copy-start(bf16[1024,128]{1,0:T(8,128)(2,1)S(1)} %collective-permute-done.4.rr.refs_3_) | copy-start | bytes 786436
  23.1 76.1 %collective-permute-start.8 = (bf16[1024,128]{1,0:T(8,128)(2,1)S(1)}, bf16[1024,128]{1,0:T(8,128)(2,1)}, u32[]{:S(2)}, u32[]{:S(2)}) collective-permute-start(bf16[1024,128]{1,0:T(8,128)(2,1)S(1)} %collective-permute-done.4.rr.refs_3_), channel_id=1, source_target_pairs={{0,64},{16,80},{32,96},{48,112},{64,128},{80,144},{96,160},{112,17... | collective-permute-start | bytes 786440 | tf_op jit(solution)/shard_map/ppermute | solution.py:541
  24.2 75.0 %collective-permute-start.9 = (bf16[1024,128]{1,0:T(8,128)(2,1)S(1)}, bf16[1024,128]{1,0:T(8,128)(2,1)S(1)}, u32[]{:S(2)}, u32[]{:S(2)}) collective-permute-start(bf16[1024,128]{1,0:T(8,128)(2,1)S(1)} %get-tuple-element.55), channel_id=1, source_target_pairs={{0,6},{2,8},{4,10},{6,12},{8,14},{10,0},{12,2},{14,4},{1,7},{3,9},... | collective-permute-start | bytes 786440 | tf_op jit(solution)/shard_map/ppermute | solution.py:545
  24.3 74.9 %collective-permute-start.10 = (bf16[1024,128]{1,0:T(8,128)(2,1)S(1)}, bf16[1024,128]{1,0:T(8,128)(2,1)S(1)}, u32[]{:S(2)}, u32[]{:S(2)}) collective-permute-start(bf16[1024,128]{1,0:T(8,128)(2,1)S(1)} %get-tuple-element.56), channel_id=1, source_target_pairs={{0,10},{2,12},{4,14},{6,0},{8,2},{10,4},{12,6},{14,8},{1,11},{3,13... | collective-permute-start | bytes 786440 | tf_op jit(solution)/shard_map/ppermute | solution.py:545
  28.8 70.4 %copy-start.11 = (bf16[4,16,4096]{2,1,0:T(8,128)(2,1)S(1)}, bf16[4,16,4096]{2,1,0:T(8,128)(2,1)}, u32[]{:S(2)}) copy-start(bf16[4,16,4096]{2,1,0:T(8,128)(2,1)} %q_ref.1) | copy-start | bytes 1572868
  28.8 70.4 %copy-start.12 = (bf16[4,16,256]{2,1,0:T(8,128)(2,1)S(1)}, bf16[4,16,256]{2,1,0:T(8,128)(2,1)}, u32[]{:S(2)}) copy-start(bf16[4,16,256]{2,1,0:T(8,128)(2,1)} %nk_ref.1) | copy-start | bytes 98308
  28.8 70.5 %copy-start.13 = (bf16[4,16,256]{2,1,0:T(8,128)(2,1)S(1)}, bf16[4,16,256]{2,1,0:T(8,128)(2,1)}, u32[]{:S(2)}) copy-start(bf16[4,16,256]{2,1,0:T(8,128)(2,1)} %nv_ref.1) | copy-start | bytes 98308
  28.8 70.4 %collective-permute-start.7 = (bf16[2048,128]{1,0:T(8,128)(2,1)S(1)}, bf16[2048,128]{1,0:T(8,128)(2,1)}, u32[]{:S(2)}, u32[]{:S(2)}) collective-permute-start(bf16[2048,128]{1,0:T(8,128)(2,1)S(1)} %get-tuple-element.54), channel_id=1, source_target_pairs={{0,32},{16,48},{32,0},{48,16},{64,96},{80,112},{96,64},{112,80},{1... | collective-permute-start | bytes 1572872 | tf_op jit(solution)/shard_map/ppermute | solution.py:541
  99.2 1.0 copy-start.2
  100.2 0.7 copy-start.7
  103.7 71.8 %copy-start.8 = (s32[5]{0:T(128)S(1)}, s32[5]{0:T(128)}, u32[]{:S(2)}) copy-start(s32[5]{0:T(128)} %copy-done.6) | copy-start | bytes 64
  103.7 71.7 %collective-permute-start.13 = (bf16[64,2176]{1,0:T(8,128)(2,1)S(1)}, bf16[64,2176]{1,0:T(8,128)(2,1)S(1)}, u32[]{:S(2)}, u32[]{:S(2)}) collective-permute-start(bf16[64,2176]{1,0:T(8,128)(2,1)S(1)} %decode_part.1.refs_0_), channel_id=1, source_target_pairs={{0,192},{16,208},{32,224},{48,240},{64,128},{80,144},{96,160},{112... | collective-permute-start | bytes 835592 | tf_op jit(solution)/shard_map/ppermute | solution.py:541
  103.8 71.6 %collective-permute-start.12 = (bf16[64,2176]{1,0:T(8,128)(2,1)S(1)}, bf16[64,2176]{1,0:T(8,128)(2,1)S(1)}, u32[]{:S(2)}, u32[]{:S(2)}) collective-permute-start(bf16[64,2176]{1,0:T(8,128)(2,1)S(1)} %decode_part.1.refs_0_), channel_id=1, source_target_pairs={{0,128},{16,144},{32,160},{48,176},{64,192},{80,208},{96,224},{112... | collective-permute-start | bytes 835592 | tf_op jit(solution)/shard_map/ppermute | solution.py:541
  103.9 71.5 %collective-permute-start.11 = (bf16[64,2176]{1,0:T(8,128)(2,1)S(1)}, bf16[64,2176]{1,0:T(8,128)(2,1)S(1)}, u32[]{:S(2)}, u32[]{:S(2)}) collective-permute-start(bf16[64,2176]{1,0:T(8,128)(2,1)S(1)} %decode_part.1.refs_0_), channel_id=1, source_target_pairs={{0,64},{16,80},{32,96},{48,112},{64,0},{80,16},{96,32},{112,48},{1... | collective-permute-start | bytes 835592 | tf_op jit(solution)/shard_map/ppermute | solution.py:541
  107.0 68.4 %collective-permute-start.14 = (bf16[1024,128]{1,0:T(8,128)(2,1)}, bf16[1024,128]{1,0:T(8,128)(2,1)S(1)}, u32[]{:S(2)}, u32[]{:S(2)}) collective-permute-start(bf16[1024,128]{1,0:T(8,128)(2,1)} %collective-permute-done.8.refs_3_), channel_id=1, source_target_pairs={{0,32},{16,48},{32,0},{48,16},{64,96},{80,112},{96,64},{112,80},{1... | collective-permute-start | bytes 786440 | tf_op jit(solution)/shard_map/ppermute | solution.py:541
  175.4 1.5 copy-start.18
  176.8 161.1 %copy-start.9 = (s32[5]{0:T(128)S(1)}, s32[5]{0:T(128)}, u32[]{:S(2)}) copy-start(s32[5]{0:T(128)} %copy-done.6) | copy-start | bytes 64
  176.8 156.9 %collective-permute-start.15 = (bf16[64,2176]{1,0:T(8,128)(2,1)S(1)}, bf16[64,2176]{1,0:T(8,128)(2,1)S(1)}, u32[]{:S(2)}, u32[]{:S(2)}) collective-permute-start(bf16[64,2176]{1,0:T(8,128)(2,1)S(1)} %merge.2.refs_0_), channel_id=1, source_target_pairs={{0,32},{16,48},{32,0},{48,16},{64,96},{80,112},{96,64},{112,80},{1... | collective-permute-start | bytes 835592 | tf_op jit(solution)/shard_map/ppermute | solution.py:541
  333.7 6.7 %collective-permute-start.16 = (bf16[256,2048]{1,0:T(8,128)(2,1)}, bf16[256,2048]{1,0:T(8,128)(2,1)S(1)}, u32[]{:S(2)}, u32[]{:S(2)}) collective-permute-start(bf16[256,2048]{1,0:T(8,128)(2,1)} %get-tuple-element.82), channel_id=1, source_target_pairs={{0,16},{16,0},{32,48},{48,32},{64,80},{80,64},{96,112},{112,96},{1... | collective-permute-start | bytes 3145736 | tf_op jit(solution)/shard_map/ppermute | solution.py:541
  339.0 4.9 %copy-start.3 = (bf16[64,2048]{1,0:T(8,128)(2,1)}, bf16[64,2048]{1,0:T(8,128)(2,1)S(1)}, u32[]{:S(2)}) copy-start(bf16[64,2048]{1,0:T(8,128)(2,1)S(1)} %merge.3) | copy-start | bytes 786436
  340.4 3.5 %collective-permute-start.17 = (bf16[64,2048]{1,0:T(8,128)(2,1)S(1)}, bf16[64,2048]{1,0:T(8,128)(2,1)S(1)}, u32[]{:S(2)}, u32[]{:S(2)}) collective-permute-start(bf16[64,2048]{1,0:T(8,128)(2,1)S(1)} %merge.3), channel_id=1, source_target_pairs={{0,16},{16,0},{32,48},{48,32},{64,80},{80,64},{96,112},{112,96},{1... | collective-permute-start | bytes 786440 | tf_op jit(solution)/shard_map/ppermute | solution.py:541
  340.7 1.2 copy-start
  343.9 0.7 copy-start.14
